TPU v7x, 512 devices: a whole 4x8x8 slice. The times are simulated.
512 devices in a mesh: edge: 128 (over z, y, core), mp: 4 (over x).
Axes of the slice: x: 4, y: 8, z: 8, core: 2. Of those that a mesh axis runs over, the one named last changes fastest.
Arguments:
- edge_feat: bfloat16 [262144, 512], P('edge', 'mp'), may hold values from -6 to 6
- mirror_rows: int32 [262144], P('edge'), may hold values from 0 to 2047, as said below
- edge_slot: int32 [2048, 128], P('edge'), may hold values from 0 to 15
- group_owner: int32 [8192, 1], P('edge'), may hold values from 0 to 127; in each aligned block of 64 rows (0 to 63, 64 to 127, ...) at most 2 rows name the same one
- group_window: int32 [8192], P('edge'), may hold values from 0 to 127
- up_edge: bfloat16 [512, 512], P(None, 'mp'), may hold values from -0.25 to 0.25
- down_edge: bfloat16 [512, 512], P('mp'), may hold values from -0.25 to 0.25
- mix_self: bfloat16 [512, 512], P(None, 'mp'), may hold values from -0.1875 to 0.1875
- mix_mirror: bfloat16 [512, 512], P(None, 'mp'), may hold values from -0.1875 to 0.1875
- up_atom: bfloat16 [512, 512], P(None, 'mp'), may hold values from -0.25 to 0.25
- down_atom: bfloat16 [512, 512], P('mp'), may hold values from -0.25 to 0.25
- atom_gain: float32 [512], replicated, may hold values from 0.1 to 1.9
Outputs:
- atom_out: bfloat16 [262144, 512], P('edge', 'mp')
Inputs may be any that keep to these rules, and one draw needn't show every extreme that they name: Within each block of 2048 rows mirror_rows is a permutation; the partner block holds its inverse permutation, so the matching of reverse edges is symmetric. `group_owner`: among the 64 groups of one device, no owner is named more than 2 times, and in every draw some device names some owner exactly 2 times.
All inputs are finite; a program needn't handle non-finite values.
Results may differ from a plain program's by a relative error of at most 0.014.
Values may be sent and summed in bfloat16 or wider, within the bound.
No kernel may reach another device: no remote copies, remote signals or barrier semaphores. Data moves between devices by JAX's collectives and lax.ppermute only.
A program may use at most 64 MiB of HBM per device.

v0:
```python
import jax
import jax.numpy as jnp
from jax import lax
from jax.sharding import PartitionSpec as P

A_DEV = 2048
GR = 32
AW = 16


def from_partner(block, axis, distance):
    count = lax.axis_size(axis)
    route = []
    for low in range(count):
        high = low | 1 << distance
        if high != low and high < count:
            route += [(low, high), (high, low)]
    return lax.ppermute(block, axis, route)


def body(
    edge_feat,
    mirror_rows,
    edge_slot,
    group_owner,
    group_window,
    up_edge,
    down_edge,
    mix_self,
    mix_mirror,
    up_atom,
    down_atom,
    atom_gain,
):
    rows = edge_feat.shape[0]
    local_width = edge_feat.shape[1]
    edge_pre = jnp.dot(
        lax.all_gather(edge_feat, "mp", axis=1, tiled=True),
        up_edge,
        preferred_element_type=jnp.float32,
    )
    edge_hidden = jax.nn.silu(edge_pre).astype(jnp.bfloat16)
    partial_value = jnp.dot(edge_hidden, down_edge, preferred_element_type=jnp.float32)
    summed = lax.psum_scatter(
        partial_value.astype(jnp.bfloat16), "mp", scatter_dimension=1, tiled=True
    ).astype(jnp.float32)
    edge_one = (edge_feat.astype(jnp.float32) + summed).astype(jnp.bfloat16)
    top_bit = lax.axis_size("edge").bit_length() - 2
    partner_rows = from_partner(edge_one, "edge", top_bit)
    reverse = jnp.take(partner_rows, mirror_rows, axis=0)
    total = jnp.dot(
        lax.all_gather(edge_one, "mp", axis=1, tiled=True),
        mix_self,
        preferred_element_type=jnp.float32,
    )
    mixed = total + jnp.dot(
        lax.all_gather(reverse, "mp", axis=1, tiled=True),
        mix_mirror,
        preferred_element_type=jnp.float32,
    )
    edge_two = (edge_one.astype(jnp.float32) + jax.nn.silu(mixed)).astype(jnp.bfloat16)
    groups = rows // GR
    slots = edge_slot.reshape(groups, GR)
    window_rows = jnp.arange(AW, dtype=jnp.int32)
    selector = (slots[:, None, :] == window_rows[None, :, None]).astype(jnp.bfloat16)
    grouped = edge_two.reshape(groups, GR, local_width)
    partial_blocks = jnp.einsum(
        "gae,gef->gaf", selector, grouped, preferred_element_type=jnp.float32
    )
    owners = lax.axis_size("edge")
    capacity = max(2, 2 * groups // owners)
    owner = group_owner[:, 0]
    order = jnp.arange(groups, dtype=jnp.int32)
    earlier = (owner[:, None] == owner[None, :]) & (order[:, None] > order[None, :])
    rank = jnp.sum(earlier.astype(jnp.int32), axis=1)
    position = owner * capacity + rank
    send_blocks = (
        jnp.zeros((owners * capacity, AW, local_width), jnp.float32)
        .at[position]
        .set(partial_blocks)
    )
    send_windows = (
        jnp.full((owners * capacity,), -1.0, jnp.float32)
        .at[position]
        .set(group_window.astype(jnp.float32))
    )
    got_blocks, got_windows = (
        lax.all_to_all(
            send_blocks.astype(jnp.bfloat16), "edge", split_axis=0, concat_axis=0, tiled=True
        ).astype(send_blocks.dtype),
        lax.all_to_all(
            send_windows.astype(jnp.bfloat16), "edge", split_axis=0, concat_axis=0, tiled=True
        ).astype(send_windows.dtype),
    )
    windows = A_DEV // AW
    placing = (got_windows[None, :] == jnp.arange(windows, dtype=jnp.float32)[:, None]).astype(
        jnp.float32
    )
    flat_blocks = got_blocks.reshape(owners * capacity, AW * local_width)
    atom_total = jnp.dot(
        placing, flat_blocks, precision=lax.Precision.HIGHEST, preferred_element_type=jnp.float32
    )
    atom_sum = atom_total.reshape(A_DEV, local_width).astype(jnp.bfloat16)
    atom_full = lax.all_gather(atom_sum, "mp", axis=1, tiled=True).astype(jnp.float32)
    scale = lax.rsqrt(jnp.mean(atom_full * atom_full, axis=1, keepdims=True) + 1e-06)
    normed = (atom_full * scale * atom_gain).astype(jnp.bfloat16)
    atom_hidden = jax.nn.silu(jnp.dot(normed, up_atom, preferred_element_type=jnp.float32)).astype(
        jnp.bfloat16
    )
    atom_partial = jnp.dot(atom_hidden, down_atom, preferred_element_type=jnp.float32)
    atom_update = lax.psum_scatter(
        atom_partial.astype(jnp.bfloat16), "mp", scatter_dimension=1, tiled=True
    ).astype(jnp.float32)
    return (atom_sum.astype(jnp.float32) + atom_update).astype(jnp.bfloat16)


def solution(mesh):
    in_specs = (
        P("edge", "mp"),
        P("edge"),
        P("edge", None),
        P("edge", None),
        P("edge"),
        P(None, "mp"),
        P("mp", None),
        P(None, "mp"),
        P(None, "mp"),
        P(None, "mp"),
        P("mp", None),
        P(),
    )
    out_specs = P("edge", "mp")
    return jax.shard_map(body, mesh=mesh, in_specs=in_specs, out_specs=out_specs, check_vma=False)
```

profile of v0, /device:TPU:1, one launch (start us, length us, event | category | flops | bytes accessed | tf_op | source)
XLA Modules:
  0.0 323.2 jit_solution(15392101213659013230)
XLA Ops:
  6.5 0.7 all-gather.5.cloned.1.call-update
  7.3 46.6 %all-gather.5.cloned.1.call-done = bf16[2048,512]{1,0:T(8,128)(2,1)} async-done(((bf16[2048,128]{1,0:T(8,128)(2,1)}), bf16[2048,512]{1,0:T(8,128)(2,1)}) %all-gather.5.cloned.1.call-update) | async-done | bytes 2097168 | tf_op jit(solution)/shard_map/all_gather | solution.py:38
  53.9 3.5 %convolution_convert_fusion.1 = bf16[2048,512]{1,0:T(8,128)(2,1)S(1)} fusion(bf16[128,512]{1,0:T(8,128)(2,1)S(1)} %copy-done, bf16[2048,512]{1,0:T(8,128)(2,1)} %all-gather.5.cloned.1.call-done, bf16[512,128]{1,0:T(8,128)(2,1)} %param.17), kind=kOutput, calls=%fused_computation.9 | convolution fusion | flops 539230208 | bytes 4456448 | tf_op jit(solution)/shard_map/dot_general | solution.py:43
  57.4 2.5 copy.15
  60.0 37.1 %reduce-scatter.7.cloned.1.call-done = bf16[128,2048]{1,0:T(8,128)(2,1)} async-done(((bf16[512,2048]{1,0:T(8,128)(2,1)}), bf16[128,2048]{1,0:T(8,128)(2,1)}) %reduce-scatter.7.cloned.1.call-update) | async-done | bytes 524304
  97.0 1.3 copy.16
  98.4 0.9 add_convert_fusion.2
  99.4 7.7 %collective-permute-start = (bf16[2048,128]{1,0:T(8,128)(2,1)}, bf16[2048,128]{1,0:T(8,128)(2,1)S(1)}, u32[]{:S(2)}, u32[]{:S(2)}) collective-permute-start(bf16[2048,128]{1,0:T(8,128)(2,1)} %add_convert_fusion.2), channel_id=1, source_target_pairs={{0,256},{256,0},{4,260},{260,4},{8,264},{264,8},{12,268},{268,12},... | collective-permute-start | bytes 1572872 | tf_op jit(solution)/shard_map/ppermute | solution.py:18
  107.2 15.1 %collective-permute-done = bf16[2048,128]{1,0:T(8,128)(2,1)S(1)} collective-permute-done((bf16[2048,128]{1,0:T(8,128)(2,1)}, bf16[2048,128]{1,0:T(8,128)(2,1)S(1)}, u32[]{:S(2)}, u32[]{:S(2)}) %collective-permute-start) | collective-permute-done | bytes 524320 | tf_op jit(solution)/shard_map/ppermute | solution.py:18
  122.2 6.2 %gather_fusion = bf16[2048,128]{1,0:T(8,128)(2,1)S(1)} fusion(bf16[2048,128]{1,0:T(8,128)(2,1)S(1)} %collective-permute-done, s32[2048]{0:T(1024)S(1)} %fusion.19), kind=kCustom, calls=%fused_computation | custom fusion | bytes 1056768 | tf_op jit(solution)/shard_map/jit(_take)/gather | solution.py:50
  128.4 1.1 broadcast_select_fusion
  129.8 0.8 scatter_custom_fusion
  130.6 0.8 all_to_all.12
  131.4 22.3 %all-to-all-start = ((bf16[128,2,1]{1,2,0:T(2,128)(2,1)}), bf16[128,2,1]{1,2,0:T(2,128)(2,1)S(1)}, u32[]{:S(2)}, u32[]{:S(2)}) async-start(bf16[128,2,1]{1,2,0:T(2,128)(2,1)} %all_to_all.12), calls=%async_computation | async-start | bytes 131072 | tf_op jit(solution)/shard_map/all_to_all | solution.py:91
  153.8 2.3 fusion.27
  156.1 25.1 %all-gather.9.cloned.1.call-done = bf16[2048,512]{1,0:T(8,128)(2,1)} async-done(((bf16[2048,128]{1,0:T(8,128)(2,1)}), bf16[2048,512]{1,0:T(8,128)(2,1)}) %all-gather.9.cloned.1.call-update) | async-done | bytes 2097168 | tf_op jit(solution)/shard_map/all_gather | solution.py:57
  181.2 2.3 add_convert_fusion.1
  183.5 0.3 fusion.15
  183.9 2.5 scatter_fusion
  186.4 1.1 convert_element_type.85
  187.5 15.2 %all-to-all-start.1 = ((bf16[256,16,128]{2,1,0:T(8,128)(2,1)}), bf16[256,16,128]{2,1,0:T(8,128)(2,1)S(1)}, u32[]{:S(2)}, u32[]{:S(2)}) async-start(bf16[256,16,128]{2,1,0:T(8,128)(2,1)} %convert_element_type.85), calls=%async_computation.1 | async-start | bytes 2097152 | tf_op jit(solution)/shard_map/all_to_all | solution.py:88
  202.7 0.2 convert_reduce_fusion
  203.1 30.5 %all-to-all-done.1 = bf16[256,16,128]{2,1,0:T(8,128)(2,1)S(1)} async-done(((bf16[256,16,128]{2,1,0:T(8,128)(2,1)}), bf16[256,16,128]{2,1,0:T(8,128)(2,1)S(1)}, u32[]{:S(2)}, u32[]{:S(2)}) %all-to-all-start.1) | async-done | bytes 1048608 | tf_op jit(solution)/shard_map/all_to_all | solution.py:88
  233.6 0.3 convolution_convert_fusion.2
  234.0 1.0 convert_element_type.87
  235.1 32.3 %all-gather.11.cloned.1.call-done = bf16[2048,512]{1,0:T(8,128)(2,1)} async-done(((bf16[2048,128]{1,0:T(8,128)(2,1)}), bf16[2048,512]{1,0:T(8,128)(2,1)}) %all-gather.11.cloned.1.call-update) | async-done | bytes 2097168 | tf_op jit(solution)/shard_map/all_gather | solution.py:104
  267.4 2.2 fusion
  269.6 3.3 %convolution_convert_fusion = bf16[2048,512]{1,0:T(8,128)(2,1)} fusion(bf16[128,512]{1,0:T(8,128)(2,1)S(1)} %copy-done.9, bf16[512,128]{1,0:T(8,128)(2,1)S(1)} %copy-done.10, bf16[2048,512]{1,0:T(8,128)(2,1)S(1)} %copy-done.4, f32[512]{0:T(512)S(1)} %copy-done.11, f32[2048]{0:T(1024)S(1)} %add_rsqrt_fusion), kind=kOutput, calls=%fused_computation.8 | convolution fusion | flops 543424512 | bytes 4466688 | tf_op jit(solution)/shard_map/dot_general | solution.py:110
  273.0 3.9 %copy.17 = bf16[2048,512]{0,1:T(8,128)(2,1)} copy(bf16[2048,512]{1,0:T(8,128)(2,1)} %convolution_convert_fusion) | data formatting | bytes 4194304
  276.9 37.1 %reduce-scatter.9.cloned.1.call-done = bf16[128,2048]{1,0:T(8,128)(2,1)} async-done(((bf16[512,2048]{1,0:T(8,128)(2,1)}), bf16[128,2048]{1,0:T(8,128)(2,1)}) %reduce-scatter.9.cloned.1.call-update) | async-done | bytes 524304
  314.0 1.3 copy.18
  315.4 0.9 add_convert_fusion
  (51 shorter events, 0.9 us)
Async XLA Ops:
  6.5 47.4 %copy-start = (bf16[128,512]{1,0:T(8,128)(2,1)S(1)}, bf16[128,512]{1,0:T(8,128)(2,1)}, u32[]{:S(2)}) copy-start(bf16[128,512]{1,0:T(8,128)(2,1)} %param.18) | copy-start | bytes 393220
  6.5 47.4 %all-gather.5.cloned.1.call-start = ((), (), s32[]{:S(2)}) async-start(), calls=%async_computation.4 | async-start | bytes 2621440 | tf_op jit(solution)/shard_map/all_gather | solution.py:38
  7.3 89.8 %reduce-scatter.7.cloned.1.call-start = ((), (), s32[]{:S(2)}) async-start(), calls=%async_computation.8 | async-start | bytes 2621440
  59.9 38.5 %copy-start.2 = (bf16[2048,128]{1,0:T(8,128)(2,1)S(1)}, bf16[2048,128]{1,0:T(8,128)(2,1)}, u32[]{:S(2)}) copy-start(bf16[2048,128]{1,0:T(8,128)(2,1)} %param.12) | copy-start | bytes 1572868
  59.9 47.2 %copy-start.6 = (s32[2048]{0:T(1024)S(1)}, s32[2048]{0:T(1024)}, u32[]{:S(2)}) copy-start(s32[2048]{0:T(1024)} %param.13) | copy-start | bytes 24580
  59.9 93.8 %all-gather.7.cloned.1.call-start = ((), (), s32[]{:S(2)}) async-start(), calls=%async_computation.5 | async-start | bytes 2621440 | tf_op jit(solution)/shard_map/all_gather | solution.py:52
  99.3 81.9 %all-gather.9.cloned.1.call-start = ((), (), s32[]{:S(2)}) async-start(), calls=%async_computation.6 | async-start | bytes 2621440 | tf_op jit(solution)/shard_map/all_gather | solution.py:57
  99.4 22.9 %collective-permute-start = (bf16[2048,128]{1,0:T(8,128)(2,1)}, bf16[2048,128]{1,0:T(8,128)(2,1)S(1)}, u32[]{:S(2)}, u32[]{:S(2)}) collective-permute-start(bf16[2048,128]{1,0:T(8,128)(2,1)} %add_convert_fusion.2), channel_id=1, source_target_pairs={{0,256},{256,0},{4,260},{260,4},{8,264},{264,8},{12,268},{268,12},... | collective-permute-start | bytes 1572872 | tf_op jit(solution)/shard_map/ppermute | solution.py:18
  107.1 22.5 %copy-start.12 = (s32[64]{0:T(128)S(1)}, s32[64]{0:T(128)}, u32[]{:S(2)}) copy-start(s32[64]{0:T(128)} %param.16) | copy-start | bytes 772
  107.2 22.5 %copy-start.13 = (s32[64,1]{0,1:T(1,128)S(1)}, s32[64,1]{0,1:T(1,128)}, u32[]{:S(2)}) copy-start(s32[64,1]{0,1:T(1,128)} %param.15) | copy-start | bytes 772
  107.2 46.5 %copy-start.7 = (s32[16,128]{1,0:T(8,128)S(1)}, s32[16,128]{1,0:T(8,128)}, u32[]{:S(2)}) copy-start(s32[16,128]{1,0:T(8,128)} %param.14) | copy-start | bytes 24580
  107.2 46.6 %copy-start.5 = (bf16[512,128]{1,0:T(8,128)(2,1)S(1)}, bf16[512,128]{1,0:T(8,128)(2,1)}, u32[]{:S(2)}) copy-start(bf16[512,128]{1,0:T(8,128)(2,1)} %param.19) | copy-start | bytes 393220
  129.6 51.6 %copy-start.3 = (bf16[2048,128]{1,0:T(8,128)(2,1)S(1)}, bf16[2048,128]{1,0:T(8,128)(2,1)}, u32[]{:S(2)}) copy-start(bf16[2048,128]{1,0:T(8,128)(2,1)} %add_convert_fusion.2) | copy-start | bytes 1572868
  129.6 51.6 %copy-start.8 = (bf16[512,128]{1,0:T(8,128)(2,1)S(1)}, bf16[512,128]{1,0:T(8,128)(2,1)}, u32[]{:S(2)}) copy-start(bf16[512,128]{1,0:T(8,128)(2,1)} %param.20) | copy-start | bytes 393220
  131.4 56.1 %all-to-all-start = ((bf16[128,2,1]{1,2,0:T(2,128)(2,1)}), bf16[128,2,1]{1,2,0:T(2,128)(2,1)S(1)}, u32[]{:S(2)}, u32[]{:S(2)}) async-start(bf16[128,2,1]{1,2,0:T(2,128)(2,1)} %all_to_all.12), calls=%async_computation | async-start | bytes 131072 | tf_op jit(solution)/shard_map/all_to_all | solution.py:91
  187.5 46.1 %all-to-all-start.1 = ((bf16[256,16,128]{2,1,0:T(8,128)(2,1)}), bf16[256,16,128]{2,1,0:T(8,128)(2,1)S(1)}, u32[]{:S(2)}, u32[]{:S(2)}) async-start(bf16[256,16,128]{2,1,0:T(8,128)(2,1)} %convert_element_type.85), calls=%async_computation.1 | async-start | bytes 2097152 | tf_op jit(solution)/shard_map/all_to_all | solution.py:88
  202.7 64.7 %all-gather.11.cloned.1.call-start = ((), (), s32[]{:S(2)}) async-start(), calls=%async_computation.7 | async-start | bytes 2621440 | tf_op jit(solution)/shard_map/all_gather | solution.py:104
  233.9 35.7 %copy-start.9 = (bf16[128,512]{1,0:T(8,128)(2,1)S(1)}, bf16[128,512]{1,0:T(8,128)(2,1)}, u32[]{:S(2)}) copy-start(bf16[128,512]{1,0:T(8,128)(2,1)} %param.22) | copy-start | bytes 393220
  234.0 35.7 %copy-start.10 = (bf16[512,128]{1,0:T(8,128)(2,1)S(1)}, bf16[512,128]{1,0:T(8,128)(2,1)}, u32[]{:S(2)}) copy-start(bf16[512,128]{1,0:T(8,128)(2,1)} %param.21) | copy-start | bytes 393220
  234.0 35.7 %copy-start.11 = (f32[512]{0:T(512)S(1)}, f32[512]{0:T(512)}, u32[]{:S(2)}) copy-start(f32[512]{0:T(512)} %param.23) | copy-start | bytes 6148
  235.0 79.0 %reduce-scatter.9.cloned.1.call-start = ((), (), s32[]{:S(2)}) async-start(), calls=%async_computation.9 | async-start | bytes 2621440
  267.4 2.3 copy-start.4
  276.9 38.5 %copy-start.1 = (bf16[2048,128]{1,0:T(8,128)(2,1)S(1)}, bf16[2048,128]{1,0:T(8,128)(2,1)}, u32[]{:S(2)}) copy-start(bf16[2048,128]{1,0:T(8,128)(2,1)} %convert_element_type.87) | copy-start | bytes 1572868
Sparse Core Ops, SparseCore 0:
  9.5 44.4 all-gather.4
  60.0 36.9 reduce-scatter.6
  99.4 38.6 all-gather.6
  140.3 40.8 all-gather.8
  235.2 32.1 all-gather.10
  277.1 36.9 reduce-scatter.8
where the time goes:
time: 324 us; the launch traced here: 323 us
  waiting for transfers between devices  225 us (69%)
  starting transfers between devices  45.4 us (14%)
  local copies, waits for them, and re-layouts  20.7 us (6%)
  between operations  13.8 us (4%)
  matrix products  12 us (4%)
  other arithmetic  6.74 us (2%)
    unnamed x8, waiting for transfers between devices  75 us
    all_gather x1, waiting for transfers between devices, body(): lax.all_gather(edge_feat, 'mp', axis=1, tiled=True)  46.6 us
    all_gather x1, waiting for transfers between devices, body(): lax.all_gather(atom_sum, 'mp', axis=1, tiled=True).astype(jnp.float32)  32.3 us
    all_to_all x1, waiting for transfers between devices, body(): lax.all_to_all(send_blocks.astype(jnp.bfloat16), 'edge', split_axis=0, co...  30.5 us
    all_gather x1, waiting for transfers between devices, body(): lax.all_gather(reverse, 'mp', axis=1, tiled=True)  25.1 us
    all_to_all x1, starting transfers between devices, body(): lax.all_to_all(send_windows.astype(jnp.bfloat16), 'edge', split_axis=0, c...  22.3 us
    all_to_all x1, starting transfers between devices, body(): lax.all_to_all(send_blocks.astype(jnp.bfloat16), 'edge', split_axis=0, co...  15.2 us
    ppermute x1, waiting for transfers between devices, from_partner(): return lax.ppermute(block, axis, route)  15.1 us
  transfers between devices with their start and end apart: 9, of which 7 were waited for; matrix products, arithmetic and copies ran while one was open for 5% of the time, Pallas kernels for 0%

commit v1 on v0

v1 whole, which is shorter than its diff:
```python
import jax
import jax.numpy as jnp
from jax import lax
from jax.experimental import pallas as pl
from jax.experimental.pallas import tpu as pltpu
from jax.sharding import PartitionSpec as P

A_DEV = 2048
GR = 32
AW = 16
MP = 4
F = 128
D = 512
ROWS = 2048
OWN = ROWS // MP
GROUPS = ROWS // GR
OWNERS = 128
CAP = 2
VMEM = pltpu.VMEM
LIMIT = 48 * 1024 * 1024


def silu(v):
    return v / (1.0 + jnp.exp(-v))


def vmem_spec():
    return pl.BlockSpec(memory_space=pltpu.VMEM)


def smem_spec():
    return pl.BlockSpec(memory_space=pltpu.SMEM)


def params():
    return pltpu.CompilerParams(vmem_limit_bytes=LIMIT)


def mm(a, b):
    return jnp.dot(a, b, preferred_element_type=jnp.float32)


def gather_kernel(rows_ref, mirror_ref, out_ref):
    step = 256
    lanes = lax.broadcasted_iota(jnp.int32, (step, F), 1)

    @pl.loop(0, ROWS // step)
    def _(k):
        picks = []
        for half in range(step // F):
            line = mirror_ref[pl.ds(k * (step // F) + half, 1), :]
            picks.append(jnp.broadcast_to(line, (F, F)).T)
        pick = jnp.concatenate(picks, axis=0)
        hot = jnp.concatenate(
            [
                jnp.where(pick == lanes + j * F, 1.0, 0.0).astype(jnp.bfloat16)
                for j in range(ROWS // F)
            ],
            axis=1,
        )
        got = mm(hot, rows_ref[...])
        out_ref[pl.ds(pl.multiple_of(k * step, step), step), :] = got.astype(jnp.bfloat16)


def gather_rows(rows, mirror):
    return pl.pallas_call(
        gather_kernel,
        out_shape=jax.ShapeDtypeStruct((ROWS, F), jnp.bfloat16),
        in_specs=[vmem_spec()] * 2,
        out_specs=vmem_spec(),
        compiler_params=params(),
        name="gather_rows",
    )(rows, mirror.reshape(ROWS // F, F))


def windows_kernel(owner_ref, window_ref, out_ref):
    owner = owner_ref[...]
    hot = lax.broadcasted_iota(jnp.int32, (OWNERS, GROUPS), 0) == owner
    before = lax.broadcasted_iota(jnp.int32, (GROUPS, GROUPS), 0) < lax.broadcasted_iota(
        jnp.int32, (GROUPS, GROUPS), 1
    )
    rank = mm(
        jnp.where(hot, 1.0, 0.0).astype(jnp.bfloat16),
        jnp.where(before, 1.0, 0.0).astype(jnp.bfloat16),
    )
    value = window_ref[...].astype(jnp.float32) + 1.0
    lane = lax.broadcasted_iota(jnp.int32, (OWNERS, F), 1)
    out = jnp.full((OWNERS, F), -1.0, jnp.float32)
    for r in range(CAP):
        mine = jnp.where(hot & (rank == float(r)), value, 0.0)
        out = jnp.where(lane == r, jnp.sum(mine, axis=1, keepdims=True) - 1.0, out)
    out_ref[...] = out.astype(jnp.bfloat16)


def send_windows(owner, window):
    return pl.pallas_call(
        windows_kernel,
        out_shape=jax.ShapeDtypeStruct((OWNERS, F), jnp.bfloat16),
        in_specs=[vmem_spec()] * 2,
        out_specs=vmem_spec(),
        compiler_params=params(),
        name="send_windows",
    )(owner.reshape(1, GROUPS), window.reshape(1, GROUPS))


def wide(ref, start, pair):
    return jnp.concatenate(
        [ref[2 * pair, start : start + D, :], ref[2 * pair + 1, start : start + D, :]], axis=1
    )


def down_wide(ref, start, pair):
    blocks = [
        jnp.concatenate([ref[m, start + j * F : start + (j + 1) * F, :] for j in (2 * pair, 2 * pair + 1)], axis=1)
        for m in range(MP)
    ]
    return jnp.concatenate(blocks, axis=0)


def side_by_side(ref):
    return jnp.concatenate([ref[m] for m in range(MP)], axis=1)


def mlp(inputs, base, w_ref, up_at, down_at):
    hidden = jnp.concatenate(
        [silu(mm(inputs, wide(w_ref, up_at, p))).astype(jnp.bfloat16) for p in range(2)], axis=1
    )
    return [
        (base[:, 2 * F * p : 2 * F * (p + 1)].astype(jnp.float32) + mm(hidden, down_wide(w_ref, down_at, p))).astype(
            jnp.bfloat16
        )
        for p in range(2)
    ]


def edge_kernel(own_ref, rev_ref, slot_ref, w_ref, out_ref):
    own = side_by_side(own_ref)
    rev = side_by_side(rev_ref)
    one = jnp.concatenate(mlp(own, own, w_ref, 0, D), axis=1)
    reverse = jnp.concatenate(mlp(rev, rev, w_ref, 0, D), axis=1)
    groups = OWN // GR
    at = lax.broadcasted_iota(jnp.int32, (groups * AW, OWN), 0)
    target = slot_ref[...] + (lax.broadcasted_iota(jnp.int32, (1, OWN), 1) // GR) * AW
    pick = jnp.where(at == target, 1.0, 0.0).astype(jnp.bfloat16)
    for p in range(2):
        mixed = mm(one, wide(w_ref, 2 * D, p)) + mm(reverse, wide(w_ref, 3 * D, p))
        two = (one[:, 2 * F * p : 2 * F * (p + 1)].astype(jnp.float32) + silu(mixed)).astype(jnp.bfloat16)
        sums = mm(pick, two).astype(jnp.bfloat16)
        out_ref[2 * p] = sums[:, :F]
        out_ref[2 * p + 1] = sums[:, F:]


def edge_stage(own, rev, slots, weights):
    return pl.pallas_call(
        edge_kernel,
        out_shape=jax.ShapeDtypeStruct((MP, OWN // GR * AW, F), jnp.bfloat16),
        in_specs=[vmem_spec()] * 4,
        out_specs=vmem_spec(),
        compiler_params=params(),
        name="edge_stage",
    )(own, rev, slots, weights)


def place_kernel(owner_ref, blocks_ref, out_ref, seen_ref):
    @pl.loop(0, OWNERS, unroll=8)
    def _(o):
        seen_ref[o] = 0

    out_ref[...] = jnp.zeros_like(out_ref)

    @pl.loop(0, GROUPS, unroll=4)
    def _(g):
        owner = owner_ref[g]
        rank = seen_ref[owner]
        seen_ref[owner] = rank + 1
        out_ref[owner * CAP + rank] = blocks_ref[g]


def place(owner, blocks):
    return pl.pallas_call(
        place_kernel,
        out_shape=jax.ShapeDtypeStruct((OWNERS * CAP, AW, F), jnp.bfloat16),
        in_specs=[smem_spec(), vmem_spec()],
        out_specs=vmem_spec(),
        scratch_shapes=[pltpu.SMEM((OWNERS,), jnp.int32)],
        compiler_params=params(),
        name="place_groups",
    )(owner, blocks)


def atom_kernel(x_ref, gain_ref, w_ref, out_ref):
    base = side_by_side(x_ref)
    full = base.astype(jnp.float32)
    scale = lax.rsqrt(jnp.mean(full * full, axis=1, keepdims=True) + 1e-06)
    normed = (full * scale * gain_ref[...]).astype(jnp.bfloat16)
    out = mlp(normed, base, w_ref, 0, D)
    for p in range(2):
        out_ref[2 * p] = out[p][:, :F]
        out_ref[2 * p + 1] = out[p][:, F:]


def atom_stage(x, gain, weights):
    return pl.pallas_call(
        atom_kernel,
        out_shape=jax.ShapeDtypeStruct((MP, OWN, F), jnp.bfloat16),
        in_specs=[vmem_spec()] * 3,
        out_specs=vmem_spec(),
        compiler_params=params(),
        name="atom_stage",
    )(x, gain.reshape(1, D), weights)


def transpose_mp(x):
    return lax.all_to_all(x, "mp", split_axis=0, concat_axis=0, tiled=True)


def columns(down):
    return [down[:, j * F : (j + 1) * F] for j in range(MP)]


def body(
    edge_feat,
    mirror_rows,
    edge_slot,
    group_owner,
    group_window,
    up_edge,
    down_edge,
    mix_self,
    mix_mirror,
    up_atom,
    down_atom,
    atom_gain,
):
    half = OWNERS // 2
    partner = lax.ppermute(edge_feat, "edge", [(e, e ^ half) for e in range(OWNERS)])
    edge_w = lax.all_gather(
        jnp.concatenate([up_edge, *columns(down_edge), mix_self, mix_mirror], axis=0), "mp", axis=0
    )
    atom_w = lax.all_gather(jnp.concatenate([up_atom, *columns(down_atom)], axis=0), "mp", axis=0)
    owner = group_owner.reshape(GROUPS)
    got_windows = lax.all_to_all(
        send_windows(owner, group_window).reshape(OWNERS, 1, F), "edge", split_axis=0, concat_axis=0, tiled=True
    )
    own = transpose_mp(edge_feat.reshape(MP, OWN, F))
    rev = transpose_mp(gather_rows(partner, mirror_rows).reshape(MP, OWN, F))
    me = lax.axis_index("mp")
    slots = lax.dynamic_slice(edge_slot, (me * (OWN // F), 0), (OWN // F, F)).reshape(1, OWN)
    partial = edge_stage(own, rev, slots, edge_w)
    blocks = transpose_mp(partial).reshape(GROUPS, AW, F)
    got = lax.all_to_all(place(owner, blocks), "edge", split_axis=0, concat_axis=0, tiled=True)
    win = got_windows[:, 0, :CAP].reshape(1, OWNERS * CAP).astype(jnp.float32)
    windows = A_DEV // AW
    placing = (win == jnp.arange(windows, dtype=jnp.float32)[:, None]).astype(jnp.bfloat16)
    atom_sum = jnp.dot(
        placing, got.reshape(OWNERS * CAP, AW * F), preferred_element_type=jnp.float32
    ).astype(jnp.bfloat16)
    x = transpose_mp(atom_sum.reshape(MP, OWN, F))
    return transpose_mp(atom_stage(x, atom_gain, atom_w)).reshape(A_DEV, F)


def solution(mesh):
    in_specs = (
        P("edge", "mp"),
        P("edge"),
        P("edge", None),
        P("edge", None),
        P("edge"),
        P(None, "mp"),
        P("mp", None),
        P(None, "mp"),
        P(None, "mp"),
        P(None, "mp"),
        P("mp", None),
        P(),
    )
    out_specs = P("edge", "mp")
    return jax.shard_map(body, mesh=mesh, in_specs=in_specs, out_specs=out_specs, check_vma=False)
```

time: 324 us -> 181 us (0.56)
  waiting for transfers between devices: 225 us -> 75.9 us
  Pallas kernels: 0 us -> 11.9 us
  matrix products: 12 us -> 0.33 us
  blocking collectives: 0 us -> 10.8 us
  starting transfers between devices: 45.4 us -> 54 us
  local copies, waits for them, and re-layouts: 20.7 us -> 12.9 us
  other arithmetic: 6.74 us -> 0.19 us
    all_gather x4 -> x2, waiting for transfers between devices: 104 us -> 0.74 us  [the longest x1 0.71 us: body(): lax.all_gather(jnp.concatenate([up_edge, *columns(down_edge), mix_self, m...]
    unnamed x8 -> x2, waiting for transfers between devices: 75 us -> 0.03 us
    all_to_all x2 -> x6, waiting for transfers between devices: 30.5 us -> 68.1 us  [the longest x1 29.8 us: body(): lax.all_to_all(place(owner, blocks), 'edge', split_axis=0, concat_axis=0,...]
    pallas_call x0 -> x5, Pallas kernels: none -> 11.9 us  [the longest x1 4.67 us: gather_rows(): pl.pallas_call(gather_kernel, out_shape=jax.ShapeDtypeStruct((ROWS, F), j...]
    dot_general x6 -> x1, matrix products: 12 us -> 0.33 us  [body(): jnp.dot(placing, got.reshape(OWNERS * CAP, AW * F), preferred_element_typ...]
    all_to_all x0 -> x1, blocking collectives: none -> 10.8 us  [transpose_mp(): return lax.all_to_all(x, 'mp', split_axis=0, concat_axis=0, tiled=True)]
    ppermute x1, waiting for transfers between devices: 15.1 us -> 7.02 us  [body(): lax.ppermute(edge_feat, 'edge', [(e, e ^ half) for e in range(OWNERS)])]
    gather x1 -> x0, local copies, waits for them, and re-layouts: 6.18 us -> none  [body(): reverse = jnp.take(partner_rows, mirror_rows, axis=0)]
  transfers between devices with their start and end apart: 9 -> 9, of which waited for: 7 -> 7; matrix products, arithmetic and copies ran while one was open for 5% -> 1% of each run, Pallas kernels for 0% -> 4%
where the time goes in v1:
time: 181 us; the launch traced here: 180 us
  waiting for transfers between devices  75.9 us (42%)
  starting transfers between devices  54 us (30%)
  between operations  13.6 us (8%)
  local copies, waits for them, and re-layouts  12.9 us (7%)
  Pallas kernels  11.9 us (7%)
  blocking collectives  10.8 us (6%)
    all_to_all x1, waiting for transfers between devices, body(): lax.all_to_all(place(owner, blocks), 'edge', split_axis=0, concat_axis=0,...  29.8 us
    all_to_all x4, waiting for transfers between devices, transpose_mp(): return lax.all_to_all(x, 'mp', split_axis=0, concat_axis=0, tiled=True)  29.1 us
    all_to_all x1, starting transfers between devices, body(): lax.all_to_all(send_windows(owner, group_window).reshape(OWNERS, 1, F), '...  20.8 us
    all_to_all x4, starting transfers between devices, transpose_mp(): return lax.all_to_all(x, 'mp', split_axis=0, concat_axis=0, tiled=True)  16 us
    ppermute x1, starting transfers between devices, body(): lax.ppermute(edge_feat, 'edge', [(e, e ^ half) for e in range(OWNERS)])  11.5 us
    all_to_all x1, blocking collectives, transpose_mp(): return lax.all_to_all(x, 'mp', split_axis=0, concat_axis=0, tiled=True)  10.8 us
    unnamed x33, local copies, waits for them, and re-layouts  10.1 us
    all_to_all x1, waiting for transfers between devices, body(): lax.all_to_all(send_windows(owner, group_window).reshape(OWNERS, 1, F), '...  9.26 us
  transfers between devices with their start and end apart: 9, of which 7 were waited for; matrix products, arithmetic and copies ran while one was open for 1% of the time, Pallas kernels for 4%

profile of v1, /device:TPU:1, one launch (start us, length us, event | category | flops | bytes accessed | tf_op | source)
XLA Modules:
  0.0 179.6 jit_solution(14525675813858933749)
XLA Ops:
  6.5 0.9 constant_dynamic-update-slice_fusion.2
  7.5 0.8 slice_dynamic-update-slice_fusion.7
  8.3 0.8 slice_dynamic-update-slice_fusion.6
  9.0 0.8 slice_dynamic-update-slice_fusion.5
  9.8 0.8 slice_dynamic-update-slice_fusion.4
  10.6 0.9 constant_dynamic-update-slice_fusion.1
  11.5 0.9 constant_dynamic-update-slice_fusion
  12.4 0.8 copy-done.7
  13.2 11.5 %collective-permute-start = (bf16[2048,128]{1,0:T(8,128)(2,1)}, bf16[2048,128]{1,0:T(8,128)(2,1)S(1)}, u32[]{:S(2)}, u32[]{:S(2)}) collective-permute-start(bf16[2048,128]{1,0:T(8,128)(2,1)} %param.12), channel_id=1, source_target_pairs={{0,256},{4,260},{8,264},{12,268},{16,272},{20,276},{24,280},{28,28... | collective-permute-start | bytes 1572872 | tf_op jit(solution)/shard_map/ppermute | solution.py:236
  24.7 4.0 %all-to-all-start.1 = ((bf16[4,512,128]{2,1,0:T(8,128)(2,1)}), bf16[4,512,128]{2,1,0:T(8,128)(2,1)S(1)}, u32[]{:S(2)}, u32[]{:S(2)}) async-start(bf16[4,512,128]{2,1,0:T(8,128)(2,1)} %bitcast.29), calls=%async_computation.1 | async-start | bytes 1048576 | tf_op jit(solution)/shard_map/all_to_all | solution.py:214
  28.7 7.0 %collective-permute-done.rows_ref = bf16[2048,128]{1,0:T(8,128)(2,1)S(1)} collective-permute-done((bf16[2048,128]{1,0:T(8,128)(2,1)}, bf16[2048,128]{1,0:T(8,128)(2,1)S(1)}, u32[]{:S(2)}, u32[]{:S(2)}) %collective-permute-start) | collective-permute-done | bytes 524320 | tf_op jit(solution)/shard_map/ppermute | solution.py:236
  35.8 4.7 %gather_rows.1 = bf16[2048,128]{1,0:T(8,128)(2,1)} custom-call(bf16[2048,128]{1,0:T(8,128)(2,1)S(1)} %collective-permute-done.rows_ref, s32[16,128]{1,0:T(8,128)S(1)} %bitcast.21), custom_call_target="tpu_custom_call" | custom-call | tf_op jit(solution)/shard_map/gather_rows/pallas_call | solution.py:66
  40.4 4.9 %all-to-all-start.2 = ((bf16[4,512,128]{2,1,0:T(8,128)(2,1)}), bf16[4,512,128]{2,1,0:T(8,128)(2,1)S(1)}, u32[]{:S(2)}, u32[]{:S(2)}) async-start(bf16[4,512,128]{2,1,0:T(8,128)(2,1)} %bitcast.6), calls=%async_computation.2 | async-start | bytes 1048576 | tf_op jit(solution)/shard_map/all_to_all | solution.py:214
  45.4 14.9 %all-to-all-done.2.rev_ref = bf16[4,512,128]{2,1,0:T(8,128)(2,1)S(1)} async-done(((bf16[4,512,128]{2,1,0:T(8,128)(2,1)}), bf16[4,512,128]{2,1,0:T(8,128)(2,1)S(1)}, u32[]{:S(2)}, u32[]{:S(2)}) %all-to-all-start.2) | async-done | bytes 524320 | tf_op jit(solution)/shard_map/all_to_all | solution.py:214
  60.3 0.7 all-gather.5.cloned.1.call-done
  61.0 1.6 copy-done.1
  62.6 3.8 %edge_stage.1 = bf16[4,256,128]{2,1,0:T(8,128)(2,1)} custom-call(bf16[4,512,128]{2,1,0:T(8,128)(2,1)S(1)} %all-to-all-done.1.own_ref, bf16[4,512,128]{2,1,0:T(8,128)(2,1)S(1)} %all-to-all-done.2.rev_ref, s32[1,512]{1,0:T(1,128)S(1)} %bitcast.22, bf16[4,2048,128]{2,1,0:T(8,128)(2,1)S(1)} %bitcast.17), custom_call_target="tpu_custom_call" | custom-call | tf_op jit(solution)/shard_map/edge_stage/pallas_call | solution.py:154
  66.4 3.5 %all-to-all-start.3 = ((bf16[4,256,128]{2,1,0:T(8,128)(2,1)}), bf16[4,256,128]{2,1,0:T(8,128)(2,1)S(1)}, u32[]{:S(2)}, u32[]{:S(2)}) async-start(bf16[4,256,128]{2,1,0:T(8,128)(2,1)} %edge_stage.1), calls=%async_computation.3 | async-start | bytes 524288 | tf_op jit(solution)/shard_map/all_to_all | solution.py:214
  70.9 4.9 %all-to-all-done.3 = bf16[4,256,128]{2,1,0:T(8,128)(2,1)S(1)} async-done(((bf16[4,256,128]{2,1,0:T(8,128)(2,1)}), bf16[4,256,128]{2,1,0:T(8,128)(2,1)S(1)}, u32[]{:S(2)}, u32[]{:S(2)}) %all-to-all-start.3) | async-done | bytes 262176 | tf_op jit(solution)/shard_map/all_to_all | solution.py:214
  75.8 20.8 %all-to-all-start = ((bf16[128,1,128]{2,1,0:T(2,128)(2,1)}), bf16[128,1,128]{2,1,0:T(2,128)(2,1)S(1)}, u32[]{:S(2)}, u32[]{:S(2)}) async-start(bf16[128,1,128]{2,1,0:T(2,128)(2,1)} %copy.13), calls=%async_computation | async-start | bytes 131072 | tf_op jit(solution)/shard_map/all_to_all | solution.py:242
  96.6 2.2 %place_groups.1 = bf16[256,16,128]{2,1,0:T(8,128)(2,1)} custom-call(s32[64]{0:T(128)S(1)} %bitcast.25, bf16[64,16,128]{2,1,0:T(8,128)(2,1)S(1)} %bitcast.19), custom_call_target="tpu_custom_call" | custom-call | tf_op jit(solution)/shard_map/place_groups/pallas_call | solution.py:180
  98.8 9.3 %all-to-all-done = bf16[128,1,128]{2,1,0:T(2,128)(2,1)S(1)} async-done(((bf16[128,1,128]{2,1,0:T(2,128)(2,1)}), bf16[128,1,128]{2,1,0:T(2,128)(2,1)S(1)}, u32[]{:S(2)}, u32[]{:S(2)}) %all-to-all-start) | async-done | bytes 32800 | tf_op jit(solution)/shard_map/all_to_all | solution.py:242
  108.1 5.8 %all-to-all-start.4 = ((bf16[256,16,128]{2,1,0:T(8,128)(2,1)}), bf16[256,16,128]{2,1,0:T(8,128)(2,1)S(1)}, u32[]{:S(2)}, u32[]{:S(2)}) async-start(bf16[256,16,128]{2,1,0:T(8,128)(2,1)} %place_groups.1), calls=%async_computation.4 | async-start | bytes 2097152 | tf_op jit(solution)/shard_map/all_to_all | solution.py:251
  114.0 0.7 copy-done.8
  115.1 29.8 %all-to-all-done.4 = bf16[256,16,128]{2,1,0:T(8,128)(2,1)S(1)} async-done(((bf16[256,16,128]{2,1,0:T(8,128)(2,1)}), bf16[256,16,128]{2,1,0:T(8,128)(2,1)S(1)}, u32[]{:S(2)}, u32[]{:S(2)}) %all-to-all-start.4) | async-done | bytes 1048608 | tf_op jit(solution)/shard_map/all_to_all | solution.py:251
  145.2 1.0 reshape.54
  146.2 3.5 %all-to-all-start.5 = ((bf16[4,512,128]{2,1,0:T(8,128)(2,1)}), bf16[4,512,128]{2,1,0:T(8,128)(2,1)S(1)}, u32[]{:S(2)}, u32[]{:S(2)}) async-start(bf16[4,512,128]{2,1,0:T(8,128)(2,1)} %reshape.54), calls=%async_computation.5 | async-start | bytes 1048576 | tf_op jit(solution)/shard_map/all_to_all | solution.py:214
  149.7 9.3 %all-to-all-done.5.x_ref = bf16[4,512,128]{2,1,0:T(8,128)(2,1)S(1)} async-done(((bf16[4,512,128]{2,1,0:T(8,128)(2,1)}), bf16[4,512,128]{2,1,0:T(8,128)(2,1)S(1)}, u32[]{:S(2)}, u32[]{:S(2)}) %all-to-all-start.5) | async-done | bytes 524320 | tf_op jit(solution)/shard_map/all_to_all | solution.py:214
  159.0 1.2 copy-done.2
  160.2 1.0 atom_stage.1
  161.2 10.8 %all_to_all.35 = bf16[4,512,128]{2,1,0:T(8,128)(2,1)S(1)} all-to-all(bf16[4,512,128]{2,1,0:T(8,128)(2,1)S(1)} %atom_stage.1), channel_id=1, replica_groups=mesh['edge'=128,'mp'=4] {'mp'}, dimensions={0} | all-to-all | bytes 1048576 | tf_op jit(solution)/shard_map/all_to_all | solution.py:214
  172.0 0.8 copy.30
  (35 shorter events, 1.8 us)
Async XLA Ops:
  6.5 38.8 %copy-start = (s32[16,128]{1,0:T(8,128)S(1)}, s32[16,128]{1,0:T(8,128)}, u32[]{:S(2)}) copy-start(s32[16,128]{1,0:T(8,128)} %param.14) | copy-start | bytes 24580
  6.5 29.2 %copy-start.3 = (s32[2048]{0:T(1024)S(1)}, s32[2048]{0:T(1024)}, u32[]{:S(2)}) copy-start(s32[2048]{0:T(1024)} %param.13) | copy-start | bytes 24580
  6.5 54.5 %all-gather.5.cloned.1.call-start = ((), (), s32[]{:S(2)}) async-start(), calls=%async_computation.7 | async-start | bytes 2621440 | tf_op jit(solution)/shard_map/all_gather | solution.py:237
  12.4 0.8 copy-start.7
  13.2 22.5 %collective-permute-start = (bf16[2048,128]{1,0:T(8,128)(2,1)}, bf16[2048,128]{1,0:T(8,128)(2,1)S(1)}, u32[]{:S(2)}, u32[]{:S(2)}) collective-permute-start(bf16[2048,128]{1,0:T(8,128)(2,1)} %param.12), channel_id=1, source_target_pairs={{0,256},{4,260},{8,264},{12,268},{16,272},{20,276},{24,280},{28,28... | collective-permute-start | bytes 1572872 | tf_op jit(solution)/shard_map/ppermute | solution.py:236
  24.7 15.7 %all-to-all-start.1 = ((bf16[4,512,128]{2,1,0:T(8,128)(2,1)}), bf16[4,512,128]{2,1,0:T(8,128)(2,1)S(1)}, u32[]{:S(2)}, u32[]{:S(2)}) async-start(bf16[4,512,128]{2,1,0:T(8,128)(2,1)} %bitcast.29), calls=%async_computation.1 | async-start | bytes 1048576 | tf_op jit(solution)/shard_map/all_to_all | solution.py:214
  40.4 19.9 %all-to-all-start.2 = ((bf16[4,512,128]{2,1,0:T(8,128)(2,1)}), bf16[4,512,128]{2,1,0:T(8,128)(2,1)S(1)}, u32[]{:S(2)}, u32[]{:S(2)}) async-start(bf16[4,512,128]{2,1,0:T(8,128)(2,1)} %bitcast.6), calls=%async_computation.2 | async-start | bytes 1048576 | tf_op jit(solution)/shard_map/all_to_all | solution.py:214
  45.4 24.6 %copy-start.5 = (s32[64,1]{0,1:T(1,128)S(1)}, s32[64,1]{0,1:T(1,128)}, u32[]{:S(2)}) copy-start(s32[64,1]{0,1:T(1,128)} %param.15) | copy-start | bytes 772
  45.4 24.6 %copy-start.6 = (s32[64]{0:T(128)S(1)}, s32[64]{0:T(128)}, u32[]{:S(2)}) copy-start(s32[64]{0:T(128)} %param.16) | copy-start | bytes 772
  61.0 1.6 copy-start.1
  66.4 47.4 %copy-start.9 = (bf16[512,128]{1,0:T(8,128)(2,1)S(1)}, bf16[512,128]{1,0:T(8,128)(2,1)}, u32[]{:S(2)}) copy-start(bf16[512,128]{1,0:T(8,128)(2,1)} %param.21) | copy-start | bytes 393220
  66.4 9.4 %all-to-all-start.3 = ((bf16[4,256,128]{2,1,0:T(8,128)(2,1)}), bf16[4,256,128]{2,1,0:T(8,128)(2,1)S(1)}, u32[]{:S(2)}, u32[]{:S(2)}) async-start(bf16[4,256,128]{2,1,0:T(8,128)(2,1)} %edge_stage.1), calls=%async_computation.3 | async-start | bytes 524288 | tf_op jit(solution)/shard_map/all_to_all | solution.py:214
  70.0 43.9 %copy-start.10 = (bf16[128,512]{1,0:T(8,128)(2,1)S(1)}, bf16[128,512]{1,0:T(8,128)(2,1)}, u32[]{:S(2)}) copy-start(bf16[128,512]{1,0:T(8,128)(2,1)} %param.22) | copy-start | bytes 393220
  75.8 32.3 %all-to-all-start = ((bf16[128,1,128]{2,1,0:T(2,128)(2,1)}), bf16[128,1,128]{2,1,0:T(2,128)(2,1)S(1)}, u32[]{:S(2)}, u32[]{:S(2)}) async-start(bf16[128,1,128]{2,1,0:T(2,128)(2,1)} %copy.13), calls=%async_computation | async-start | bytes 131072 | tf_op jit(solution)/shard_map/all_to_all | solution.py:242
  108.1 36.8 %all-to-all-start.4 = ((bf16[256,16,128]{2,1,0:T(8,128)(2,1)}), bf16[256,16,128]{2,1,0:T(8,128)(2,1)S(1)}, u32[]{:S(2)}, u32[]{:S(2)}) async-start(bf16[256,16,128]{2,1,0:T(8,128)(2,1)} %place_groups.1), calls=%async_computation.4 | async-start | bytes 2097152 | tf_op jit(solution)/shard_map/all_to_all | solution.py:251
  113.8 35.9 %all-gather.7.cloned.1.call-start = ((), (), s32[]{:S(2)}) async-start(), calls=%async_computation.8 | async-start | bytes 1310720 | tf_op jit(solution)/shard_map/all_gather | solution.py:240
  114.0 45.0 %copy-start.4 = (f32[512]{0:T(512)S(1)}, f32[512]{0:T(512)}, u32[]{:S(2)}) copy-start(f32[512]{0:T(512)} %param.23) | copy-start | bytes 6148
  114.0 0.7 copy-start.8
  146.2 12.8 %all-to-all-start.5 = ((bf16[4,512,128]{2,1,0:T(8,128)(2,1)}), bf16[4,512,128]{2,1,0:T(8,128)(2,1)S(1)}, u32[]{:S(2)}, u32[]{:S(2)}) async-start(bf16[4,512,128]{2,1,0:T(8,128)(2,1)} %reshape.54), calls=%async_computation.5 | async-start | bytes 1048576 | tf_op jit(solution)/shard_map/all_to_all | solution.py:214
  159.0 1.2 copy-start.2
Sparse Core Ops, SparseCore 0:
  13.3 47.6 all-gather.4
  116.8 27.4 all-gather.6

commit v2 on v1

--- a/solution.py
+++ b/solution.py
@@ -16,8 +16,10 @@
 GROUPS = ROWS // GR
 OWNERS = 128
 CAP = 2
+HEAD = 8
 VMEM = pltpu.VMEM
 LIMIT = 48 * 1024 * 1024
+ALL_VMEM = 63 * 1024 * 1024
 
 
 def silu(v):
@@ -41,7 +43,7 @@
 
 
 def gather_kernel(rows_ref, mirror_ref, out_ref):
-    step = 256
+    step = 1024
     lanes = lax.broadcasted_iota(jnp.int32, (step, F), 1)
 
     @pl.loop(0, ROWS // step)
@@ -103,6 +105,40 @@
     )(owner.reshape(1, GROUPS), window.reshape(1, GROUPS))
 
 
+def pack_kernel(*refs):
+    *sources, out_ref, held, sems = refs
+    copies = []
+    for k, source in enumerate(sources):
+        if source.shape[0] == D:
+            moves = [(source, held.at[pl.ds(k * D, D)])]
+        else:
+            moves = [
+                (source.at[:, pl.ds(j * F, F)], held.at[pl.ds(k * D + j * F, F)]) for j in range(MP)
+            ]
+        for source_part, part in moves:
+            copies.append(pltpu.make_async_copy(source_part, part, sems.at[len(copies)]))
+    for copy in copies:
+        copy.start()
+    for copy in copies:
+        copy.wait()
+    whole = pltpu.make_async_copy(held, out_ref, sems.at[len(copies)])
+    whole.start()
+    whole.wait()
+
+
+def pack(*weights, limit):
+    rows = len(weights) * D
+    return pl.pallas_call(
+        pack_kernel,
+        out_shape=jax.ShapeDtypeStruct((rows, F), jnp.bfloat16),
+        in_specs=[pl.BlockSpec(memory_space=pl.ANY)] * len(weights),
+        out_specs=pl.BlockSpec(memory_space=pl.ANY),
+        scratch_shapes=[pltpu.VMEM((rows, F), jnp.bfloat16), pltpu.SemaphoreType.DMA((len(weights) * MP + 1,))],
+        compiler_params=pltpu.CompilerParams(vmem_limit_bytes=limit),
+        name="pack_weights",
+    )(*weights)
+
+
 def wide(ref, start, pair):
     return jnp.concatenate(
         [ref[2 * pair, start : start + D, :], ref[2 * pair + 1, start : start + D, :]], axis=1
@@ -161,31 +197,78 @@
     )(own, rev, slots, weights)
 
 
-def place_kernel(owner_ref, blocks_ref, out_ref, seen_ref):
+def place_kernel(owner_ref, window_ref, blocks_ref, out_ref, seen_ref):
     @pl.loop(0, OWNERS, unroll=8)
     def _(o):
         seen_ref[o] = 0
 
-    out_ref[...] = jnp.zeros_like(out_ref)
+    out_ref[:, : CAP * AW, :] = jnp.zeros((OWNERS, CAP * AW, F), jnp.bfloat16)
+    out_ref[:, CAP * AW :, :] = jnp.full((OWNERS, HEAD, F), -1.0, jnp.bfloat16)
+    line = lax.broadcasted_iota(jnp.int32, (HEAD, F), 0)
 
     @pl.loop(0, GROUPS, unroll=4)
     def _(g):
         owner = owner_ref[g]
         rank = seen_ref[owner]
         seen_ref[owner] = rank + 1
-        out_ref[owner * CAP + rank] = blocks_ref[g]
-
-
-def place(owner, blocks):
+        out_ref[owner, pl.ds(pl.multiple_of(rank * AW, AW), AW), :] = blocks_ref[g]
+        head = out_ref[owner, CAP * AW :, :].astype(jnp.float32)
+        head = jnp.where(line == rank, window_ref[g].astype(jnp.float32), head)
+        out_ref[owner, CAP * AW :, :] = head.astype(jnp.bfloat16)
+
+
+def place(owner, window, blocks):
     return pl.pallas_call(
         place_kernel,
-        out_shape=jax.ShapeDtypeStruct((OWNERS * CAP, AW, F), jnp.bfloat16),
-        in_specs=[smem_spec(), vmem_spec()],
+        out_shape=jax.ShapeDtypeStruct((OWNERS, CAP * AW + HEAD, F), jnp.bfloat16),
+        in_specs=[smem_spec(), smem_spec(), vmem_spec()],
         out_specs=vmem_spec(),
         scratch_shapes=[pltpu.SMEM((OWNERS,), jnp.int32)],
         compiler_params=params(),
         name="place_groups",
-    )(owner, blocks)
+    )(owner, window, blocks)
+
+
+def collect_kernel(got_ref, out_ref, wide_ref, sum_ref):
+    period = CAP * AW + HEAD
+    wide_ref[...] = got_ref[...].astype(jnp.float32).reshape(OWNERS * period, F)
+    lanes = lax.broadcasted_iota(jnp.int32, (OWNERS, F), 1).astype(jnp.float32)
+    placing = jnp.concatenate(
+        [
+            jnp.where(wide_ref[pl.ds(CAP * AW + r, OWNERS, stride=period), :] == lanes, 1.0, 0.0).T
+            for r in range(CAP)
+        ],
+        axis=1,
+    ).astype(jnp.bfloat16)
+    for a in range(0, AW, 2):
+        rows = jnp.concatenate(
+            [
+                jnp.concatenate(
+                    [wide_ref[pl.ds(r * AW + b, OWNERS, stride=period), :] for b in (a, a + 1)], axis=1
+                )
+                for r in range(CAP)
+            ],
+            axis=0,
+        ).astype(jnp.bfloat16)
+        sums = mm(placing, rows)
+        sum_ref[pl.ds(a, A_DEV // AW, stride=AW), :] = sums[:, :F]
+        sum_ref[pl.ds(a + 1, A_DEV // AW, stride=AW), :] = sums[:, F:]
+    out_ref[...] = sum_ref[...].astype(jnp.bfloat16).reshape(MP, OWN, F)
+
+
+def collect(got):
+    return pl.pallas_call(
+        collect_kernel,
+        out_shape=jax.ShapeDtypeStruct((MP, OWN, F), jnp.bfloat16),
+        in_specs=[vmem_spec()],
+        out_specs=vmem_spec(),
+        scratch_shapes=[
+            pltpu.VMEM((OWNERS * (CAP * AW + HEAD), F), jnp.float32),
+            pltpu.VMEM((A_DEV, F), jnp.float32),
+        ],
+        compiler_params=params(),
+        name="collect_blocks",
+    )(got)
 
 
 def atom_kernel(x_ref, gain_ref, w_ref, out_ref):
@@ -212,10 +295,6 @@
 
 def transpose_mp(x):
     return lax.all_to_all(x, "mp", split_axis=0, concat_axis=0, tiled=True)
-
-
-def columns(down):
-    return [down[:, j * F : (j + 1) * F] for j in range(MP)]
 
 
 def body(
@@ -235,27 +314,20 @@
     half = OWNERS // 2
     partner = lax.ppermute(edge_feat, "edge", [(e, e ^ half) for e in range(OWNERS)])
     edge_w = lax.all_gather(
-        jnp.concatenate([up_edge, *columns(down_edge), mix_self, mix_mirror], axis=0), "mp", axis=0
-    )
-    atom_w = lax.all_gather(jnp.concatenate([up_atom, *columns(down_atom)], axis=0), "mp", axis=0)
+        pack(up_edge, down_edge, mix_self, mix_mirror, limit=ALL_VMEM), "mp", axis=0
+    )
     owner = group_owner.reshape(GROUPS)
-    got_windows = lax.all_to_all(
-        send_windows(owner, group_window).reshape(OWNERS, 1, F), "edge", split_axis=0, concat_axis=0, tiled=True
-    )
     own = transpose_mp(edge_feat.reshape(MP, OWN, F))
     rev = transpose_mp(gather_rows(partner, mirror_rows).reshape(MP, OWN, F))
     me = lax.axis_index("mp")
     slots = lax.dynamic_slice(edge_slot, (me * (OWN // F), 0), (OWN // F, F)).reshape(1, OWN)
     partial = edge_stage(own, rev, slots, edge_w)
+    partial, up_atom, down_atom = lax.optimization_barrier((partial, up_atom, down_atom))
+    atom_w = lax.all_gather(pack(up_atom, down_atom, limit=LIMIT), "mp", axis=0)
     blocks = transpose_mp(partial).reshape(GROUPS, AW, F)
-    got = lax.all_to_all(place(owner, blocks), "edge", split_axis=0, concat_axis=0, tiled=True)
-    win = got_windows[:, 0, :CAP].reshape(1, OWNERS * CAP).astype(jnp.float32)
-    windows = A_DEV // AW
-    placing = (win == jnp.arange(windows, dtype=jnp.float32)[:, None]).astype(jnp.bfloat16)
-    atom_sum = jnp.dot(
-        placing, got.reshape(OWNERS * CAP, AW * F), preferred_element_type=jnp.float32
-    ).astype(jnp.bfloat16)
-    x = transpose_mp(atom_sum.reshape(MP, OWN, F))
+    sent = place(owner, group_window, blocks)
+    got = lax.all_to_all(sent, "edge", split_axis=0, concat_axis=0, tiled=True)
+    x = transpose_mp(collect(got))
     return transpose_mp(atom_stage(x, atom_gain, atom_w)).reshape(A_DEV, F)
 
 

time: 181 us -> 163 us (0.901)
  starting transfers between devices: 54 us -> 43.4 us
  local copies, waits for them, and re-layouts: 12.9 us -> 3.64 us
  blocking collectives: 10.8 us -> 18.8 us
  waiting for transfers between devices: 75.9 us -> 68.4 us
  Pallas kernels: 11.9 us -> 14.6 us
    all_to_all x1 -> x2, blocking collectives: 10.8 us -> 18.8 us  [transpose_mp(): return lax.all_to_all(x, 'mp', split_axis=0, concat_axis=0, tiled=True)]
    all_to_all x2 -> x1, starting transfers between devices: 26.6 us -> 19.5 us  [body(): got = lax.all_to_all(sent, 'edge', split_axis=0, concat_axis=0, tiled=True)]
    unnamed x33 -> x19, local copies, waits for them, and re-layouts: 10.1 us -> 3.64 us
    all_to_all x4 -> x3, waiting for transfers between devices: 29.1 us -> 24.1 us  [transpose_mp(): return lax.all_to_all(x, 'mp', split_axis=0, concat_axis=0, tiled=True)]
    pallas_call x2 -> x4, Pallas kernels: 2.41 us -> 7.18 us  [the longest x2 3.04 us: pack(): pl.pallas_call(pack_kernel, out_shape=jax.ShapeDtypeStruct((rows, F), jnp...]
    all_to_all x2 -> x1, waiting for transfers between devices: 39.1 us -> 35 us  [body(): got = lax.all_to_all(sent, 'edge', split_axis=0, concat_axis=0, tiled=True)]
    all_to_all x4 -> x3, starting transfers between devices: 16 us -> 12.4 us  [transpose_mp(): return lax.all_to_all(x, 'mp', split_axis=0, concat_axis=0, tiled=True)]
  transfers between devices with their start and end apart: 9 -> 7, of which waited for: 7 -> 5; matrix products, arithmetic and copies ran while one was open for 1% -> 0% of each run, Pallas kernels for 4% -> 4%
where the time goes in v2:
time: 163 us; the launch traced here: 162 us
  waiting for transfers between devices  68.4 us (42%)
  starting transfers between devices  43.4 us (27%)
  blocking collectives  18.8 us (12%)
  Pallas kernels  14.6 us (9%)
  between operations  13.5 us (8%)
  local copies, waits for them, and re-layouts  3.64 us (2%)
    all_to_all x1, waiting for transfers between devices, body(): got = lax.all_to_all(sent, 'edge', split_axis=0, concat_axis=0, tiled=True)  35 us
    all_to_all x3, waiting for transfers between devices, transpose_mp(): return lax.all_to_all(x, 'mp', split_axis=0, concat_axis=0, tiled=True)  24.1 us
    all_to_all x1, starting transfers between devices, body(): got = lax.all_to_all(sent, 'edge', split_axis=0, concat_axis=0, tiled=True)  19.5 us
    all_to_all x2, blocking collectives, transpose_mp(): return lax.all_to_all(x, 'mp', split_axis=0, concat_axis=0, tiled=True)  18.8 us
    all_to_all x3, starting transfers between devices, transpose_mp(): return lax.all_to_all(x, 'mp', split_axis=0, concat_axis=0, tiled=True)  12.4 us
    ppermute x1, starting transfers between devices, body(): lax.ppermute(edge_feat, 'edge', [(e, e ^ half) for e in range(OWNERS)])  11.5 us
    ppermute x1, waiting for transfers between devices, body(): lax.ppermute(edge_feat, 'edge', [(e, e ^ half) for e in range(OWNERS)])  7.01 us
    unnamed x19, local copies, waits for them, and re-layouts  3.64 us
  transfers between devices with their start and end apart: 7, of which 5 were waited for; matrix products, arithmetic and copies ran while one was open for 0% of the time, Pallas kernels for 4%

profile of v2, /device:TPU:1, one launch (start us, length us, event | category | flops | bytes accessed | tf_op | source)
XLA Modules:
  0.0 162.4 jit_solution(2688108241963196917)
XLA Ops:
  6.5 0.0 copy-start
  6.5 2.1 %pack_weights.2 = bf16[2048,128]{1,0:T(8,128)(2,1)} custom-call(bf16[512,128]{1,0:T(8,128)(2,1)} %refs_0_.1, bf16[128,512]{1,0:T(8,128)(2,1)} %refs_1_.1, bf16[512,128]{1,0:T(8,128)(2,1)} %refs_2_.1, bf16[512,128]{1,0:T(8,128)(2,1)} %refs_3_.1), custom_call_target="tpu_custom_call" | custom-call | tf_op jit(solution)/shard_map/pack_weights/pallas_call | solution.py:131
  8.6 0.0 all-gather.5.cloned.1.call-update
  8.6 11.5 %collective-permute-start = (bf16[2048,128]{1,0:T(8,128)(2,1)}, bf16[2048,128]{1,0:T(8,128)(2,1)S(1)}, u32[]{:S(2)}, u32[]{:S(2)}) collective-permute-start(bf16[2048,128]{1,0:T(8,128)(2,1)} %param.12), channel_id=1, source_target_pairs={{0,256},{4,260},{8,264},{12,268},{16,272},{20,276},{24,280},{28,28... | collective-permute-start | bytes 1572872 | tf_op jit(solution)/shard_map/ppermute | solution.py:315
  20.1 4.0 %all-to-all-start = ((bf16[4,512,128]{2,1,0:T(8,128)(2,1)}), bf16[4,512,128]{2,1,0:T(8,128)(2,1)S(1)}, u32[]{:S(2)}, u32[]{:S(2)}) async-start(bf16[4,512,128]{2,1,0:T(8,128)(2,1)} %bitcast.1), calls=%async_computation | async-start | bytes 1048576 | tf_op jit(solution)/shard_map/all_to_all | solution.py:297
  24.1 7.0 %collective-permute-done.rows_ref = bf16[2048,128]{1,0:T(8,128)(2,1)S(1)} collective-permute-done((bf16[2048,128]{1,0:T(8,128)(2,1)}, bf16[2048,128]{1,0:T(8,128)(2,1)S(1)}, u32[]{:S(2)}, u32[]{:S(2)}) %collective-permute-start) | collective-permute-done | bytes 524320 | tf_op jit(solution)/shard_map/ppermute | solution.py:315
  31.1 3.4 %gather_rows.1 = bf16[2048,128]{1,0:T(8,128)(2,1)} custom-call(bf16[2048,128]{1,0:T(8,128)(2,1)S(1)} %collective-permute-done.rows_ref, s32[16,128]{1,0:T(8,128)S(1)} %bitcast.13), custom_call_target="tpu_custom_call" | custom-call | tf_op jit(solution)/shard_map/gather_rows/pallas_call | solution.py:68
  34.5 0.0 all-to-all-done.own_ref
  34.5 4.9 %all-to-all-start.1 = ((bf16[4,512,128]{2,1,0:T(8,128)(2,1)}), bf16[4,512,128]{2,1,0:T(8,128)(2,1)S(1)}, u32[]{:S(2)}, u32[]{:S(2)}) async-start(bf16[4,512,128]{2,1,0:T(8,128)(2,1)} %bitcast.3), calls=%async_computation.1 | async-start | bytes 1048576 | tf_op jit(solution)/shard_map/all_to_all | solution.py:297
  39.5 14.9 %all-to-all-done.1.rev_ref = bf16[4,512,128]{2,1,0:T(8,128)(2,1)S(1)} async-done(((bf16[4,512,128]{2,1,0:T(8,128)(2,1)}), bf16[4,512,128]{2,1,0:T(8,128)(2,1)S(1)}, u32[]{:S(2)}, u32[]{:S(2)}) %all-to-all-start.1) | async-done | bytes 524320 | tf_op jit(solution)/shard_map/all_to_all | solution.py:297
  54.4 2.3 %all-gather.5.cloned.1.call-done = bf16[8192,128]{1,0:T(8,128)(2,1)} async-done(((bf16[2048,128]{1,0:T(8,128)(2,1)}), bf16[8192,128]{1,0:T(8,128)(2,1)}) %all-gather.5.cloned.1.call-update) | async-done | bytes 2097168 | tf_op jit(solution)/shard_map/all_gather | solution.py:316
  56.7 1.6 copy-done.1
  58.3 3.1 %edge_stage.1 = bf16[4,256,128]{2,1,0:T(8,128)(2,1)S(1)} custom-call(bf16[4,512,128]{2,1,0:T(8,128)(2,1)S(1)} %all-to-all-done.own_ref, bf16[4,512,128]{2,1,0:T(8,128)(2,1)S(1)} %all-to-all-done.1.rev_ref, s32[1,512]{1,0:T(1,128)S(1)} %bitcast.14, bf16[4,2048,128]{2,1,0:T(8,128)(2,1)S(1)} %bitcast.10), custom_call_target="tpu_custom_call" | custom-call | tf_op jit(solution)/shard_map/edge_stage/pallas_call | solution.py:190
  61.4 8.1 %all_to_all.30 = bf16[4,256,128]{2,1,0:T(8,128)(2,1)S(1)} all-to-all(bf16[4,256,128]{2,1,0:T(8,128)(2,1)S(1)} %edge_stage.1), channel_id=1, replica_groups=mesh['edge'=128,'mp'=4] {'mp'}, dimensions={0} | all-to-all | bytes 524288 | tf_op jit(solution)/shard_map/all_to_all | solution.py:297
  69.6 0.0 copy-done.8
  69.6 2.4 %place_groups.1 = bf16[128,40,128]{2,1,0:T(8,128)(2,1)} custom-call(s32[64]{0:T(128)S(1)} %bitcast.16, s32[64]{0:T(128)S(1)} %copy-done.8, bf16[64,16,128]{2,1,0:T(8,128)(2,1)S(1)} %bitcast.12), custom_call_target="tpu_custom_call" | custom-call | tf_op jit(solution)/shard_map/place_groups/pallas_call | solution.py:221
  72.0 19.5 %all-to-all-start.3 = ((bf16[128,40,128]{2,1,0:T(8,128)(2,1)}), bf16[128,40,128]{2,1,0:T(8,128)(2,1)S(1)}, u32[]{:S(2)}, u32[]{:S(2)}) async-start(bf16[128,40,128]{2,1,0:T(8,128)(2,1)} %place_groups.1), calls=%async_computation.3 | async-start | bytes 2621440 | tf_op jit(solution)/shard_map/all_to_all | solution.py:329
  91.5 0.0 all-gather.7.cloned.1.call-start
  91.5 0.0 copy-done.3
  91.5 0.0 copy-done.4
  91.5 1.0 pack_weights.3
  92.5 0.0 all-gather.7.cloned.1.call-update
  92.6 0.0 copy-start.6
  92.6 35.0 %all-to-all-done.3.got_ref = bf16[128,40,128]{2,1,0:T(8,128)(2,1)S(1)} async-done(((bf16[128,40,128]{2,1,0:T(8,128)(2,1)}), bf16[128,40,128]{2,1,0:T(8,128)(2,1)S(1)}, u32[]{:S(2)}, u32[]{:S(2)}) %all-to-all-start.3) | async-done | bytes 1310752 | tf_op jit(solution)/shard_map/all_to_all | solution.py:329
  127.5 1.7 %collect_blocks.1 = bf16[4,512,128]{2,1,0:T(8,128)(2,1)} custom-call(bf16[128,40,128]{2,1,0:T(8,128)(2,1)S(1)} %all-to-all-done.3.got_ref), custom_call_target="tpu_custom_call" | custom-call | tf_op jit(solution)/shard_map/collect_blocks/pallas_call | solution.py:260
  129.2 3.5 %all-to-all-start.4 = ((bf16[4,512,128]{2,1,0:T(8,128)(2,1)}), bf16[4,512,128]{2,1,0:T(8,128)(2,1)S(1)}, u32[]{:S(2)}, u32[]{:S(2)}) async-start(bf16[4,512,128]{2,1,0:T(8,128)(2,1)} %collect_blocks.1), calls=%async_computation.4 | async-start | bytes 1048576 | tf_op jit(solution)/shard_map/all_to_all | solution.py:297
  132.7 0.0 all-gather.7.cloned.1.call-done
  132.7 9.1 %all-to-all-done.4.x_ref = bf16[4,512,128]{2,1,0:T(8,128)(2,1)S(1)} async-done(((bf16[4,512,128]{2,1,0:T(8,128)(2,1)}), bf16[4,512,128]{2,1,0:T(8,128)(2,1)S(1)}, u32[]{:S(2)}, u32[]{:S(2)}) %all-to-all-start.4) | async-done | bytes 524320 | tf_op jit(solution)/shard_map/all_to_all | solution.py:297
  141.9 1.2 copy-done.2
  143.1 1.0 atom_stage.1
  144.1 10.7 %all_to_all.31 = bf16[4,512,128]{2,1,0:T(8,128)(2,1)S(1)} all-to-all(bf16[4,512,128]{2,1,0:T(8,128)(2,1)S(1)} %atom_stage.1), channel_id=1, replica_groups=mesh['edge'=128,'mp'=4] {'mp'}, dimensions={0} | all-to-all | bytes 1048576 | tf_op jit(solution)/shard_map/all_to_all | solution.py:297
  154.8 0.8 copy.14
  (13 shorter events, 0.0 us)
Async XLA Ops:
  6.5 33.0 %copy-start = (s32[16,128]{1,0:T(8,128)S(1)}, s32[16,128]{1,0:T(8,128)}, u32[]{:S(2)}) copy-start(s32[16,128]{1,0:T(8,128)} %param.14) | copy-start | bytes 24580
  6.5 24.6 %copy-start.5 = (s32[2048]{0:T(1024)S(1)}, s32[2048]{0:T(1024)}, u32[]{:S(2)}) copy-start(s32[2048]{0:T(1024)} %param.13) | copy-start | bytes 24580
  6.5 50.2 %all-gather.5.cloned.1.call-start = ((), (), s32[]{:S(2)}) async-start(), calls=%async_computation.6 | async-start | bytes 2621440 | tf_op jit(solution)/shard_map/all_gather | solution.py:316
  8.6 22.5 %collective-permute-start = (bf16[2048,128]{1,0:T(8,128)(2,1)}, bf16[2048,128]{1,0:T(8,128)(2,1)S(1)}, u32[]{:S(2)}, u32[]{:S(2)}) collective-permute-start(bf16[2048,128]{1,0:T(8,128)(2,1)} %param.12), channel_id=1, source_target_pairs={{0,256},{4,260},{8,264},{12,268},{16,272},{20,276},{24,280},{28,28... | collective-permute-start | bytes 1572872 | tf_op jit(solution)/shard_map/ppermute | solution.py:315
  20.1 14.4 %all-to-all-start = ((bf16[4,512,128]{2,1,0:T(8,128)(2,1)}), bf16[4,512,128]{2,1,0:T(8,128)(2,1)S(1)}, u32[]{:S(2)}, u32[]{:S(2)}) async-start(bf16[4,512,128]{2,1,0:T(8,128)(2,1)} %bitcast.1), calls=%async_computation | async-start | bytes 1048576 | tf_op jit(solution)/shard_map/all_to_all | solution.py:297
  34.5 19.9 %all-to-all-start.1 = ((bf16[4,512,128]{2,1,0:T(8,128)(2,1)}), bf16[4,512,128]{2,1,0:T(8,128)(2,1)S(1)}, u32[]{:S(2)}, u32[]{:S(2)}) async-start(bf16[4,512,128]{2,1,0:T(8,128)(2,1)} %bitcast.3), calls=%async_computation.1 | async-start | bytes 1048576 | tf_op jit(solution)/shard_map/all_to_all | solution.py:297
  56.7 1.6 copy-start.1
  58.3 11.2 %copy-start.7 = (s32[64,1]{0,1:T(1,128)S(1)}, s32[64,1]{0,1:T(1,128)}, u32[]{:S(2)}) copy-start(s32[64,1]{0,1:T(1,128)} %param.15) | copy-start | bytes 772
  58.3 11.2 %copy-start.8 = (s32[64]{0:T(128)S(1)}, s32[64]{0:T(128)}, u32[]{:S(2)}) copy-start(s32[64]{0:T(128)} %window_ref.1) | copy-start | bytes 772
  72.0 19.5 %copy-start.3 = (bf16[512,128]{1,0:T(8,128)(2,1)S(1)}, bf16[512,128]{1,0:T(8,128)(2,1)}, u32[]{:S(2)}) copy-start(bf16[512,128]{1,0:T(8,128)(2,1)} %refs_0_.2) | copy-start | bytes 393220
  72.0 19.5 %copy-start.4 = (bf16[128,512]{1,0:T(8,128)(2,1)S(1)}, bf16[128,512]{1,0:T(8,128)(2,1)}, u32[]{:S(2)}) copy-start(bf16[128,512]{1,0:T(8,128)(2,1)} %refs_1_.2) | copy-start | bytes 393220
  72.0 55.5 %all-to-all-start.3 = ((bf16[128,40,128]{2,1,0:T(8,128)(2,1)}), bf16[128,40,128]{2,1,0:T(8,128)(2,1)S(1)}, u32[]{:S(2)}, u32[]{:S(2)}) async-start(bf16[128,40,128]{2,1,0:T(8,128)(2,1)} %place_groups.1), calls=%async_computation.3 | async-start | bytes 2621440 | tf_op jit(solution)/shard_map/all_to_all | solution.py:329
  91.5 41.3 %all-gather.7.cloned.1.call-start = ((), (), s32[]{:S(2)}) async-start(), calls=%async_computation.7 | async-start | bytes 1310720 | tf_op jit(solution)/shard_map/all_gather | solution.py:326
  92.6 49.3 %copy-start.6 = (f32[512]{0:T(512)S(1)}, f32[512]{0:T(512)}, u32[]{:S(2)}) copy-start(f32[512]{0:T(512)} %param.23) | copy-start | bytes 6148
  129.2 12.6 %all-to-all-start.4 = ((bf16[4,512,128]{2,1,0:T(8,128)(2,1)}), bf16[4,512,128]{2,1,0:T(8,128)(2,1)S(1)}, u32[]{:S(2)}, u32[]{:S(2)}) async-start(bf16[4,512,128]{2,1,0:T(8,128)(2,1)} %collect_blocks.1), calls=%async_computation.4 | async-start | bytes 1048576 | tf_op jit(solution)/shard_map/all_to_all | solution.py:297
  141.9 1.2 copy-start.2
Sparse Core Ops, SparseCore 0:
  9.5 47.2 all-gather.4
  94.4 27.3 all-gather.6

commit v3 on v2

--- a/solution.py
+++ b/solution.py
@@ -13,12 +13,13 @@
 D = 512
 ROWS = 2048
 OWN = ROWS // MP
+PIECE = OWN + 2 * D
 GROUPS = ROWS // GR
 OWNERS = 128
 CAP = 2
 HEAD = 8
 VMEM = pltpu.VMEM
-LIMIT = 48 * 1024 * 1024
+LIMIT = 24 * 1024 * 1024
 ALL_VMEM = 63 * 1024 * 1024
 
 
@@ -71,6 +72,7 @@
         in_specs=[vmem_spec()] * 2,
         out_specs=vmem_spec(),
         compiler_params=params(),
+        cost_estimate=pl.CostEstimate(flops=20_000_000_000, bytes_accessed=64_000_000, transcendentals=0),
         name="gather_rows",
     )(rows, mirror.reshape(ROWS // F, F))
 
@@ -139,6 +141,56 @@
     )(*weights)
 
 
+def core_index():
+    return lax.rem(lax.axis_index("edge"), 2)
+
+
+def share_kernel(rows_ref, up_ref, down_ref, self_ref, mirror_ref, out_ref, held, sems):
+    def move(moves):
+        copies = [pltpu.make_async_copy(src, dst, sems.at[k]) for k, (src, dst) in enumerate(moves)]
+        for copy in copies:
+            copy.start()
+        for copy in copies:
+            copy.wait()
+
+    own = [(rows_ref, held.at[:, pl.ds(0, OWN)])]
+    core = core_index()
+
+    @pl.when(core == 0)
+    def _():
+        moves = list(own)
+        for m in range(MP):
+            moves.append((up_ref, held.at[m, pl.ds(OWN, D)]))
+            for j in range(MP):
+                moves.append((down_ref.at[:, pl.ds(j * F, F)], held.at[m, pl.ds(OWN + D + j * F, F)]))
+        move(moves)
+
+    @pl.when(core != 0)
+    def _():
+        moves = list(own)
+        for m in range(MP):
+            moves.append((self_ref, held.at[m, pl.ds(OWN, D)]))
+            moves.append((mirror_ref, held.at[m, pl.ds(OWN + D, D)]))
+        move(moves)
+
+    move([(held, out_ref)])
+
+
+def share(rows, *weights):
+    return pl.pallas_call(
+        share_kernel,
+        out_shape=jax.ShapeDtypeStruct((MP, PIECE, F), jnp.bfloat16),
+        in_specs=[pl.BlockSpec(memory_space=pl.ANY)] * 5,
+        out_specs=pl.BlockSpec(memory_space=pl.ANY),
+        scratch_shapes=[
+            pltpu.VMEM((MP, PIECE, F), jnp.bfloat16),
+            pltpu.SemaphoreType.DMA((1 + MP * (1 + MP),)),
+        ],
+        compiler_params=pltpu.CompilerParams(vmem_limit_bytes=ALL_VMEM),
+        name="share_rows_and_weights",
+    )(rows, *weights)
+
+
 def wide(ref, start, pair):
     return jnp.concatenate(
         [ref[2 * pair, start : start + D, :], ref[2 * pair + 1, start : start + D, :]], axis=1
@@ -157,44 +209,77 @@
     return jnp.concatenate([ref[m] for m in range(MP)], axis=1)
 
 
-def mlp(inputs, base, w_ref, up_at, down_at):
-    hidden = jnp.concatenate(
-        [silu(mm(inputs, wide(w_ref, up_at, p))).astype(jnp.bfloat16) for p in range(2)], axis=1
-    )
+def up(inputs, w_ref, at):
+    return jnp.concatenate(
+        [silu(mm(inputs, wide(w_ref, at, p))).astype(jnp.bfloat16) for p in range(2)], axis=1
+    )
+
+
+def down(hidden, base, w_ref, at):
     return [
-        (base[:, 2 * F * p : 2 * F * (p + 1)].astype(jnp.float32) + mm(hidden, down_wide(w_ref, down_at, p))).astype(
+        (base[:, 2 * F * p : 2 * F * (p + 1)].astype(jnp.float32) + mm(hidden, down_wide(w_ref, at, p))).astype(
             jnp.bfloat16
         )
         for p in range(2)
     ]
 
 
-def edge_kernel(own_ref, rev_ref, slot_ref, w_ref, out_ref):
-    own = side_by_side(own_ref)
-    rev = side_by_side(rev_ref)
-    one = jnp.concatenate(mlp(own, own, w_ref, 0, D), axis=1)
-    reverse = jnp.concatenate(mlp(rev, rev, w_ref, 0, D), axis=1)
-    groups = OWN // GR
-    at = lax.broadcasted_iota(jnp.int32, (groups * AW, OWN), 0)
-    target = slot_ref[...] + (lax.broadcasted_iota(jnp.int32, (1, OWN), 1) // GR) * AW
-    pick = jnp.where(at == target, 1.0, 0.0).astype(jnp.bfloat16)
-    for p in range(2):
-        mixed = mm(one, wide(w_ref, 2 * D, p)) + mm(reverse, wide(w_ref, 3 * D, p))
-        two = (one[:, 2 * F * p : 2 * F * (p + 1)].astype(jnp.float32) + silu(mixed)).astype(jnp.bfloat16)
-        sums = mm(pick, two).astype(jnp.bfloat16)
-        out_ref[2 * p] = sums[:, :F]
-        out_ref[2 * p + 1] = sums[:, F:]
-
-
-def edge_stage(own, rev, slots, weights):
+def edge_kernel(mine_ref, other_hbm, rev_ref, slot_ref, out_ref, other_ref, sems):
+    copies = [
+        pltpu.make_async_copy(
+            other_hbm.at[:, pl.ds(OWN + k * D, D)], other_ref.at[:, pl.ds(OWN + k * D, D)], sems.at[k]
+        )
+        for k in range(2)
+    ]
+    for copy in copies:
+        copy.start()
+
+    def run(mlp_ref, mix_ref):
+        own = jnp.concatenate([mine_ref[m, :OWN] for m in range(MP)], axis=1)
+        rev = side_by_side(rev_ref)
+        if mlp_ref is other_ref:
+            copies[0].wait()
+        own_hidden = up(own, mlp_ref, OWN)
+        rev_hidden = up(rev, mlp_ref, OWN)
+        if mlp_ref is other_ref:
+            copies[1].wait()
+        one = jnp.concatenate(down(own_hidden, own, mlp_ref, OWN + D), axis=1)
+        reverse = jnp.concatenate(down(rev_hidden, rev, mlp_ref, OWN + D), axis=1)
+        if mix_ref is other_ref:
+            copies[0].wait()
+            copies[1].wait()
+        groups = OWN // GR
+        at = lax.broadcasted_iota(jnp.int32, (groups * AW, OWN), 0)
+        target = slot_ref[...] + (lax.broadcasted_iota(jnp.int32, (1, OWN), 1) // GR) * AW
+        pick = jnp.where(at == target, 1.0, 0.0).astype(jnp.bfloat16)
+        for p in range(2):
+            mixed = mm(one, wide(mix_ref, OWN, p)) + mm(reverse, wide(mix_ref, OWN + D, p))
+            two = (one[:, 2 * F * p : 2 * F * (p + 1)].astype(jnp.float32) + silu(mixed)).astype(jnp.bfloat16)
+            sums = mm(pick, two).astype(jnp.bfloat16)
+            out_ref[2 * p] = sums[:, :F]
+            out_ref[2 * p + 1] = sums[:, F:]
+
+    core = core_index()
+
+    @pl.when(core == 0)
+    def _():
+        run(mine_ref, other_ref)
+
+    @pl.when(core != 0)
+    def _():
+        run(other_ref, mine_ref)
+
+
+def edge_stage(mine, other, rev, slots):
     return pl.pallas_call(
         edge_kernel,
         out_shape=jax.ShapeDtypeStruct((MP, OWN // GR * AW, F), jnp.bfloat16),
-        in_specs=[vmem_spec()] * 4,
-        out_specs=vmem_spec(),
+        in_specs=[vmem_spec(), pl.BlockSpec(memory_space=pl.ANY), vmem_spec(), vmem_spec()],
+        out_specs=vmem_spec(),
+        scratch_shapes=[pltpu.VMEM((MP, PIECE, F), jnp.bfloat16), pltpu.SemaphoreType.DMA((2,))],
         compiler_params=params(),
         name="edge_stage",
-    )(own, rev, slots, weights)
+    )(mine, other, rev, slots)
 
 
 def place_kernel(owner_ref, window_ref, blocks_ref, out_ref, seen_ref):
@@ -271,26 +356,31 @@
     )(got)
 
 
-def atom_kernel(x_ref, gain_ref, w_ref, out_ref):
+def atom_kernel(x_ref, gain_ref, *refs):
+    *shards, out_ref, w_ref = refs
+    me = lax.axis_index("mp")
+    for shift, shard in enumerate(shards):
+        w_ref[lax.rem(me + MP - shift, MP)] = shard[...]
     base = side_by_side(x_ref)
     full = base.astype(jnp.float32)
     scale = lax.rsqrt(jnp.mean(full * full, axis=1, keepdims=True) + 1e-06)
     normed = (full * scale * gain_ref[...]).astype(jnp.bfloat16)
-    out = mlp(normed, base, w_ref, 0, D)
+    out = down(up(normed, w_ref, 0), base, w_ref, D)
     for p in range(2):
         out_ref[2 * p] = out[p][:, :F]
         out_ref[2 * p + 1] = out[p][:, F:]
 
 
-def atom_stage(x, gain, weights):
+def atom_stage(x, gain, shards):
     return pl.pallas_call(
         atom_kernel,
         out_shape=jax.ShapeDtypeStruct((MP, OWN, F), jnp.bfloat16),
-        in_specs=[vmem_spec()] * 3,
-        out_specs=vmem_spec(),
+        in_specs=[vmem_spec()] * (2 + MP),
+        out_specs=vmem_spec(),
+        scratch_shapes=[pltpu.VMEM((MP, 2 * D, F), jnp.bfloat16)],
         compiler_params=params(),
         name="atom_stage",
-    )(x, gain.reshape(1, D), weights)
+    )(x, gain.reshape(1, D), *shards)
 
 
 def transpose_mp(x):
@@ -313,20 +403,25 @@
 ):
     half = OWNERS // 2
     partner = lax.ppermute(edge_feat, "edge", [(e, e ^ half) for e in range(OWNERS)])
-    edge_w = lax.all_gather(
-        pack(up_edge, down_edge, mix_self, mix_mirror, limit=ALL_VMEM), "mp", axis=0
-    )
     owner = group_owner.reshape(GROUPS)
-    own = transpose_mp(edge_feat.reshape(MP, OWN, F))
-    rev = transpose_mp(gather_rows(partner, mirror_rows).reshape(MP, OWN, F))
+    mine = transpose_mp(
+        share(edge_feat.reshape(MP, OWN, F), up_edge, down_edge, mix_self, mix_mirror)
+    )
+    reverse, mine = lax.optimization_barrier((gather_rows(partner, mirror_rows), mine))
+    other = lax.ppermute(mine, "edge", [(e, e ^ 1) for e in range(OWNERS)])
+    rev = transpose_mp(reverse.reshape(MP, OWN, F))
     me = lax.axis_index("mp")
     slots = lax.dynamic_slice(edge_slot, (me * (OWN // F), 0), (OWN // F, F)).reshape(1, OWN)
-    partial = edge_stage(own, rev, slots, edge_w)
-    partial, up_atom, down_atom = lax.optimization_barrier((partial, up_atom, down_atom))
-    atom_w = lax.all_gather(pack(up_atom, down_atom, limit=LIMIT), "mp", axis=0)
+    partial = edge_stage(mine, other, rev, slots)
     blocks = transpose_mp(partial).reshape(GROUPS, AW, F)
     sent = place(owner, group_window, blocks)
+    sent, up_atom, down_atom = lax.optimization_barrier((sent, up_atom, down_atom))
+    atom_pack = pack(up_atom, down_atom, limit=LIMIT)
+    atom_w = [atom_pack] + [
+        lax.ppermute(atom_pack, "mp", [(m, (m + shift) % MP) for m in range(MP)]) for shift in range(1, MP)
+    ]
     got = lax.all_to_all(sent, "edge", split_axis=0, concat_axis=0, tiled=True)
+    got, *atom_w = lax.optimization_barrier((got, *atom_w))
     x = transpose_mp(collect(got))
     return transpose_mp(atom_stage(x, atom_gain, atom_w)).reshape(A_DEV, F)
 

time: 163 us -> 147 us (0.902)
  waiting for transfers between devices: 68.4 us -> 53.6 us
  between operations: 13.5 us -> 0.16 us
  blocking collectives: 18.8 us -> 31.4 us
  local copies, waits for them, and re-layouts: 3.64 us -> 0.83 us
    all_to_all x1, waiting for transfers between devices: 35 us -> 16 us  [body(): got = lax.all_to_all(sent, 'edge', split_axis=0, concat_axis=0, tiled=True)]
    all_to_all x2 -> x3, blocking collectives: 18.8 us -> 31.4 us  [transpose_mp(): return lax.all_to_all(x, 'mp', split_axis=0, concat_axis=0, tiled=True)]
    ppermute x0 -> x4, waiting for transfers between devices: none -> 11.8 us  [the longest x3 11.8 us: body(): lax.ppermute(atom_pack, 'mp', [(m, (m + shift) % MP) for m in range(MP)])]
    ppermute x0 -> x4, starting transfers between devices: none -> 11.8 us  [the longest x3 7.81 us: body(): lax.ppermute(atom_pack, 'mp', [(m, (m + shift) % MP) for m in range(MP)])]
    all_to_all x1, starting transfers between devices: 19.5 us -> 13.6 us  [body(): got = lax.all_to_all(sent, 'edge', split_axis=0, concat_axis=0, tiled=True)]
    all_to_all x3 -> x2, starting transfers between devices: 12.4 us -> 7.51 us  [transpose_mp(): return lax.all_to_all(x, 'mp', split_axis=0, concat_axis=0, tiled=True)]
    ppermute x1, waiting for transfers between devices: 7.01 us -> 4.05 us  [body(): lax.ppermute(edge_feat, 'edge', [(e, e ^ half) for e in range(OWNERS)])]
    pallas_call x0 -> x1, Pallas kernels: none -> 2.95 us  [share(): pl.pallas_call(share_kernel, out_shape=jax.ShapeDtypeStruct((MP, PIECE, F...]
  transfers between devices with their start and end apart: 7 -> 8, of which waited for: 5 -> 7; matrix products, arithmetic and copies ran while one was open for 0% -> 0% of each run, Pallas kernels for 4% -> 5%
where the time goes in v3:
time: 147 us; the launch traced here: 146 us
  waiting for transfers between devices  53.6 us (36%)
  starting transfers between devices  44.5 us (30%)
  blocking collectives  31.4 us (21%)
  Pallas kernels  15.2 us (10%)
    all_to_all x3, blocking collectives, transpose_mp(): return lax.all_to_all(x, 'mp', split_axis=0, concat_axis=0, tiled=True)  31.4 us
    all_to_all x2, waiting for transfers between devices, transpose_mp(): return lax.all_to_all(x, 'mp', split_axis=0, concat_axis=0, tiled=True)  21.7 us
    all_to_all x1, waiting for transfers between devices, body(): got = lax.all_to_all(sent, 'edge', split_axis=0, concat_axis=0, tiled=True)  16 us
    all_to_all x1, starting transfers between devices, body(): got = lax.all_to_all(sent, 'edge', split_axis=0, concat_axis=0, tiled=True)  13.6 us
    ppermute x3, waiting for transfers between devices, body(): lax.ppermute(atom_pack, 'mp', [(m, (m + shift) % MP) for m in range(MP)])  11.8 us
    ppermute x1, starting transfers between devices, body(): lax.ppermute(edge_feat, 'edge', [(e, e ^ half) for e in range(OWNERS)])  11.6 us
    ppermute x3, starting transfers between devices, body(): lax.ppermute(atom_pack, 'mp', [(m, (m + shift) % MP) for m in range(MP)])  7.81 us
    all_to_all x2, starting transfers between devices, transpose_mp(): return lax.all_to_all(x, 'mp', split_axis=0, concat_axis=0, tiled=True)  7.51 us
  transfers between devices with their start and end apart: 8, of which 7 were waited for; matrix products, arithmetic and copies ran while one was open for 0% of the time, Pallas kernels for 5%

profile of v3, /device:TPU:1, one launch (start us, length us, event | category | flops | bytes accessed | tf_op | source)
XLA Modules:
  0.0 145.6 jit_solution(13967081198974110469)
XLA Ops:
  0.0 0.0 copy-start
  0.0 11.6 %collective-permute-start = (bf16[2048,128]{1,0:T(8,128)(2,1)}, bf16[2048,128]{1,0:T(8,128)(2,1)S(1)}, u32[]{:S(2)}, u32[]{:S(2)}) collective-permute-start(bf16[2048,128]{1,0:T(8,128)(2,1)} %param.12), channel_id=1, source_target_pairs={{0,256},{4,260},{8,264},{12,268},{16,272},{20,276},{24,280},{28,28... | collective-permute-start | bytes 1572872 | tf_op jit(solution)/shard_map/ppermute | solution.py:405
  11.6 2.9 %share_rows_and_weights.1 = bf16[4,1536,128]{2,1,0:T(8,128)(2,1)} custom-call(bf16[4,512,128]{2,1,0:T(8,128)(2,1)} %bitcast.14, bf16[512,128]{1,0:T(8,128)(2,1)} %up_ref.1, bf16[128,512]{1,0:T(8,128)(2,1)} %down_ref.1, bf16[512,128]{1,0:T(8,128)(2,1)} %self_ref.1, bf16[512,128]{1,0:T(8,128)(2,1)} %mirror_ref.1), custom_call_target="tpu_custom_call" | custom-call | tf_op jit(solution)/shard_map/share_rows_and_weights/pallas_call | solution.py:180
  14.6 0.0 copy-start.6
  14.6 4.0 %all-to-all-start = ((bf16[4,1536,128]{2,1,0:T(8,128)(2,1)}), bf16[4,1536,128]{2,1,0:T(8,128)(2,1)S(1)}, u32[]{:S(2)}, u32[]{:S(2)}) async-start(bf16[4,1536,128]{2,1,0:T(8,128)(2,1)} %share_rows_and_weights.1), calls=%async_computation | async-start | bytes 3145728 | tf_op jit(solution)/shard_map/all_to_all | solution.py:387
  18.6 4.0 %collective-permute-done.rows_ref = bf16[2048,128]{1,0:T(8,128)(2,1)S(1)} collective-permute-done((bf16[2048,128]{1,0:T(8,128)(2,1)}, bf16[2048,128]{1,0:T(8,128)(2,1)S(1)}, u32[]{:S(2)}, u32[]{:S(2)}) %collective-permute-start) | collective-permute-done | bytes 524320 | tf_op jit(solution)/shard_map/ppermute | solution.py:405
  22.6 0.0 copy-done.6
  22.6 3.4 %gather_rows.1 = bf16[2048,128]{1,0:T(8,128)(2,1)} custom-call(bf16[2048,128]{1,0:T(8,128)(2,1)S(1)} %collective-permute-done.rows_ref, s32[16,128]{1,0:T(8,128)S(1)} %bitcast.12), custom_call_target="tpu_custom_call" | custom-call | flops 20000000000 | bytes 64000000 | tf_op jit(solution)/shard_map/gather_rows/pallas_call | solution.py:69
  26.0 12.1 %all-to-all-done.mine_ref = bf16[4,1536,128]{2,1,0:T(8,128)(2,1)S(1)} async-done(((bf16[4,1536,128]{2,1,0:T(8,128)(2,1)}), bf16[4,1536,128]{2,1,0:T(8,128)(2,1)S(1)}, u32[]{:S(2)}, u32[]{:S(2)}) %all-to-all-start) | async-done | bytes 1572896 | tf_op jit(solution)/shard_map/all_to_all | solution.py:387
  38.2 4.0 %collective-permute-start.1 = (bf16[4,1536,128]{2,1,0:T(8,128)(2,1)S(1)}, bf16[4,1536,128]{2,1,0:T(8,128)(2,1)}, u32[]{:S(2)}, u32[]{:S(2)}) collective-permute-start(bf16[4,1536,128]{2,1,0:T(8,128)(2,1)S(1)} %all-to-all-done.mine_ref), channel_id=1, source_target_pairs={{0,4},{4,0},{8,12},{12,8},{16,20},{20,16},{24,28},{28,24},{32,36},... | collective-permute-start | bytes 4718600 | tf_op jit(solution)/shard_map/ppermute | solution.py:411
  42.2 3.5 %all-to-all-start.1 = ((bf16[4,512,128]{2,1,0:T(8,128)(2,1)}), bf16[4,512,128]{2,1,0:T(8,128)(2,1)S(1)}, u32[]{:S(2)}, u32[]{:S(2)}) async-start(bf16[4,512,128]{2,1,0:T(8,128)(2,1)} %bitcast.3), calls=%async_computation.1 | async-start | bytes 1048576 | tf_op jit(solution)/shard_map/all_to_all | solution.py:387
  45.7 9.6 %all-to-all-done.1.rev_ref = bf16[4,512,128]{2,1,0:T(8,128)(2,1)S(1)} async-done(((bf16[4,512,128]{2,1,0:T(8,128)(2,1)}), bf16[4,512,128]{2,1,0:T(8,128)(2,1)S(1)}, u32[]{:S(2)}, u32[]{:S(2)}) %all-to-all-start.1) | async-done | bytes 524320 | tf_op jit(solution)/shard_map/all_to_all | solution.py:387
  55.3 0.0 collective-permute-done.1.other_hbm
  55.3 4.2 %edge_stage.1 = bf16[4,256,128]{2,1,0:T(8,128)(2,1)S(1)} custom-call(bf16[4,1536,128]{2,1,0:T(8,128)(2,1)S(1)} %all-to-all-done.mine_ref, bf16[4,1536,128]{2,1,0:T(8,128)(2,1)} %collective-permute-done.1.other_hbm, bf16[4,512,128]{2,1,0:T(8,128)(2,1)S(1)} %all-to-all-done.1.rev_ref, s32[1,512]{1,0:T(1,128)S(1)} %bitcast.9), custom_call_target="tpu_custom_call" | custom-call | tf_op jit(solution)/shard_map/edge_stage/pallas_call | solution.py:274
  59.5 9.4 %all_to_all.30 = bf16[4,256,128]{2,1,0:T(8,128)(2,1)S(1)} all-to-all(bf16[4,256,128]{2,1,0:T(8,128)(2,1)S(1)} %edge_stage.1), channel_id=1, replica_groups=mesh['edge'=128,'mp'=4] {'mp'}, dimensions={0} | all-to-all | bytes 524288 | tf_op jit(solution)/shard_map/all_to_all | solution.py:387
  68.9 2.4 %place_groups.1 = bf16[128,40,128]{2,1,0:T(8,128)(2,1)} custom-call(s32[64]{0:T(128)S(1)} %bitcast.11, s32[64]{0:T(128)S(1)} %copy-done.5, bf16[64,16,128]{2,1,0:T(8,128)(2,1)S(1)} %bitcast.8), custom_call_target="tpu_custom_call" | custom-call | tf_op jit(solution)/shard_map/place_groups/pallas_call | solution.py:306
  71.3 13.6 %all-to-all-start.3 = ((bf16[128,40,128]{2,1,0:T(8,128)(2,1)}), bf16[128,40,128]{2,1,0:T(8,128)(2,1)S(1)}, u32[]{:S(2)}, u32[]{:S(2)}) async-start(bf16[128,40,128]{2,1,0:T(8,128)(2,1)} %place_groups.1), calls=%async_computation.3 | async-start | bytes 2621440 | tf_op jit(solution)/shard_map/all_to_all | solution.py:423
  84.9 0.0 copy-done.1
  84.9 0.3 pack_weights.1.refs_0_
  85.2 0.0 copy-start.3
  85.2 2.8 %collective-permute-start.4 = (bf16[1024,128]{1,0:T(8,128)(2,1)S(1)}, bf16[1024,128]{1,0:T(8,128)(2,1)S(1)}, u32[]{:S(2)}, u32[]{:S(2)}) collective-permute-start(bf16[1024,128]{1,0:T(8,128)(2,1)S(1)} %pack_weights.1.refs_0_), channel_id=1, source_target_pairs={{0,3},{1,0},{2,1},{3,2},{4,7},{5,4},{6,5},{7,6},{8,11},{9,8},{10,9... | collective-permute-start | bytes 786440 | tf_op jit(solution)/shard_map/ppermute | solution.py:421
  88.0 3.1 %collective-permute-start.3 = (bf16[1024,128]{1,0:T(8,128)(2,1)S(1)}, bf16[1024,128]{1,0:T(8,128)(2,1)S(1)}, u32[]{:S(2)}, u32[]{:S(2)}) collective-permute-start(bf16[1024,128]{1,0:T(8,128)(2,1)S(1)} %pack_weights.1.refs_0_), channel_id=1, source_target_pairs={{0,2},{1,3},{2,0},{3,1},{4,6},{5,7},{6,4},{7,5},{8,10},{9,11},{10,... | collective-permute-start | bytes 786440 | tf_op jit(solution)/shard_map/ppermute | solution.py:421
  91.2 1.9 %collective-permute-start.2 = (bf16[1024,128]{1,0:T(8,128)(2,1)S(1)}, bf16[1024,128]{1,0:T(8,128)(2,1)S(1)}, u32[]{:S(2)}, u32[]{:S(2)}) collective-permute-start(bf16[1024,128]{1,0:T(8,128)(2,1)S(1)} %pack_weights.1.refs_0_), channel_id=1, source_target_pairs={{0,1},{1,2},{2,3},{3,0},{4,5},{5,6},{6,7},{7,4},{8,9},{9,10},{10,1... | collective-permute-start | bytes 786440 | tf_op jit(solution)/shard_map/ppermute | solution.py:421
  93.1 1.0 collective-permute-done.4.refs_3_
  94.1 4.0 %collective-permute-done.3.refs_2_ = bf16[1024,128]{1,0:T(8,128)(2,1)S(1)} collective-permute-done((bf16[1024,128]{1,0:T(8,128)(2,1)S(1)}, bf16[1024,128]{1,0:T(8,128)(2,1)S(1)}, u32[]{:S(2)}, u32[]{:S(2)}) %collective-permute-start.3) | collective-permute-done | bytes 262176 | tf_op jit(solution)/shard_map/ppermute | solution.py:421
  98.1 6.8 %collective-permute-done.2.refs_1_ = bf16[1024,128]{1,0:T(8,128)(2,1)S(1)} collective-permute-done((bf16[1024,128]{1,0:T(8,128)(2,1)S(1)}, bf16[1024,128]{1,0:T(8,128)(2,1)S(1)}, u32[]{:S(2)}, u32[]{:S(2)}) %collective-permute-start.2) | collective-permute-done | bytes 262176 | tf_op jit(solution)/shard_map/ppermute | solution.py:421
  104.9 16.0 %all-to-all-done.3.got_ref = bf16[128,40,128]{2,1,0:T(8,128)(2,1)S(1)} async-done(((bf16[128,40,128]{2,1,0:T(8,128)(2,1)}), bf16[128,40,128]{2,1,0:T(8,128)(2,1)S(1)}, u32[]{:S(2)}, u32[]{:S(2)}) %all-to-all-start.3) | async-done | bytes 1310752 | tf_op jit(solution)/shard_map/all_to_all | solution.py:423
  121.0 0.9 collect_blocks.1
  121.9 11.6 %all_to_all.31.x_ref = bf16[4,512,128]{2,1,0:T(8,128)(2,1)S(1)} all-to-all(bf16[4,512,128]{2,1,0:T(8,128)(2,1)S(1)} %collect_blocks.1), channel_id=1, replica_groups=mesh['edge'=128,'mp'=4] {'mp'}, dimensions={0} | all-to-all | bytes 1048576 | tf_op jit(solution)/shard_map/all_to_all | solution.py:387
  133.5 1.0 atom_stage.1
  134.5 10.4 %all_to_all.32 = bf16[4,512,128]{2,1,0:T(8,128)(2,1)S(1)} all-to-all(bf16[4,512,128]{2,1,0:T(8,128)(2,1)S(1)} %atom_stage.1), channel_id=1, replica_groups=mesh['edge'=128,'mp'=4] {'mp'}, dimensions={0} | all-to-all | bytes 1048576 | tf_op jit(solution)/shard_map/all_to_all | solution.py:387
  144.8 0.8 copy.14
  (10 shorter events, 0.0 us)
Async XLA Ops:
  0.0 45.7 %copy-start = (s32[16,128]{1,0:T(8,128)S(1)}, s32[16,128]{1,0:T(8,128)}, u32[]{:S(2)}) copy-start(s32[16,128]{1,0:T(8,128)} %param.14) | copy-start | bytes 24580
  0.0 22.6 %collective-permute-start = (bf16[2048,128]{1,0:T(8,128)(2,1)}, bf16[2048,128]{1,0:T(8,128)(2,1)S(1)}, u32[]{:S(2)}, u32[]{:S(2)}) collective-permute-start(bf16[2048,128]{1,0:T(8,128)(2,1)} %param.12), channel_id=1, source_target_pairs={{0,256},{4,260},{8,264},{12,268},{16,272},{20,276},{24,280},{28,28... | collective-permute-start | bytes 1572872 | tf_op jit(solution)/shard_map/ppermute | solution.py:405
  14.6 8.1 %copy-start.6 = (s32[2048]{0:T(1024)S(1)}, s32[2048]{0:T(1024)}, u32[]{:S(2)}) copy-start(s32[2048]{0:T(1024)} %param.13) | copy-start | bytes 24580
  14.6 23.6 %all-to-all-start = ((bf16[4,1536,128]{2,1,0:T(8,128)(2,1)}), bf16[4,1536,128]{2,1,0:T(8,128)(2,1)S(1)}, u32[]{:S(2)}, u32[]{:S(2)}) async-start(bf16[4,1536,128]{2,1,0:T(8,128)(2,1)} %share_rows_and_weights.1), calls=%async_computation | async-start | bytes 3145728 | tf_op jit(solution)/shard_map/all_to_all | solution.py:387
  38.2 17.1 %collective-permute-start.1 = (bf16[4,1536,128]{2,1,0:T(8,128)(2,1)S(1)}, bf16[4,1536,128]{2,1,0:T(8,128)(2,1)}, u32[]{:S(2)}, u32[]{:S(2)}) collective-permute-start(bf16[4,1536,128]{2,1,0:T(8,128)(2,1)S(1)} %all-to-all-done.mine_ref), channel_id=1, source_target_pairs={{0,4},{4,0},{8,12},{12,8},{16,20},{20,16},{24,28},{28,24},{32,36},... | collective-permute-start | bytes 4718600 | tf_op jit(solution)/shard_map/ppermute | solution.py:411
  42.2 13.1 %all-to-all-start.1 = ((bf16[4,512,128]{2,1,0:T(8,128)(2,1)}), bf16[4,512,128]{2,1,0:T(8,128)(2,1)S(1)}, u32[]{:S(2)}, u32[]{:S(2)}) async-start(bf16[4,512,128]{2,1,0:T(8,128)(2,1)} %bitcast.3), calls=%async_computation.1 | async-start | bytes 1048576 | tf_op jit(solution)/shard_map/all_to_all | solution.py:387
  55.3 13.6 %copy-start.4 = (s32[64,1]{0,1:T(1,128)S(1)}, s32[64,1]{0,1:T(1,128)}, u32[]{:S(2)}) copy-start(s32[64,1]{0,1:T(1,128)} %param.15) | copy-start | bytes 772
  55.3 13.6 %copy-start.5 = (s32[64]{0:T(128)S(1)}, s32[64]{0:T(128)}, u32[]{:S(2)}) copy-start(s32[64]{0:T(128)} %window_ref.1) | copy-start | bytes 772
  71.3 13.6 %copy-start.1 = (bf16[512,128]{1,0:T(8,128)(2,1)S(1)}, bf16[512,128]{1,0:T(8,128)(2,1)}, u32[]{:S(2)}) copy-start(bf16[512,128]{1,0:T(8,128)(2,1)} %refs_0_) | copy-start | bytes 393220
  71.3 13.6 %copy-start.2 = (bf16[128,512]{1,0:T(8,128)(2,1)S(1)}, bf16[128,512]{1,0:T(8,128)(2,1)}, u32[]{:S(2)}) copy-start(bf16[128,512]{1,0:T(8,128)(2,1)} %refs_1_) | copy-start | bytes 393220
  71.3 49.6 %all-to-all-start.3 = ((bf16[128,40,128]{2,1,0:T(8,128)(2,1)}), bf16[128,40,128]{2,1,0:T(8,128)(2,1)S(1)}, u32[]{:S(2)}, u32[]{:S(2)}) async-start(bf16[128,40,128]{2,1,0:T(8,128)(2,1)} %place_groups.1), calls=%async_computation.3 | async-start | bytes 2621440 | tf_op jit(solution)/shard_map/all_to_all | solution.py:423
  85.2 48.2 %copy-start.3 = (f32[512]{0:T(512)S(1)}, f32[512]{0:T(512)}, u32[]{:S(2)}) copy-start(f32[512]{0:T(512)} %param.23) | copy-start | bytes 6148
  85.2 8.8 %collective-permute-start.4 = (bf16[1024,128]{1,0:T(8,128)(2,1)S(1)}, bf16[1024,128]{1,0:T(8,128)(2,1)S(1)}, u32[]{:S(2)}, u32[]{:S(2)}) collective-permute-start(bf16[1024,128]{1,0:T(8,128)(2,1)S(1)} %pack_weights.1.refs_0_), channel_id=1, source_target_pairs={{0,3},{1,0},{2,1},{3,2},{4,7},{5,4},{6,5},{7,6},{8,11},{9,8},{10,9... | collective-permute-start | bytes 786440 | tf_op jit(solution)/shard_map/ppermute | solution.py:421
  88.0 10.0 %collective-permute-start.3 = (bf16[1024,128]{1,0:T(8,128)(2,1)S(1)}, bf16[1024,128]{1,0:T(8,128)(2,1)S(1)}, u32[]{:S(2)}, u32[]{:S(2)}) collective-permute-start(bf16[1024,128]{1,0:T(8,128)(2,1)S(1)} %pack_weights.1.refs_0_), channel_id=1, source_target_pairs={{0,2},{1,3},{2,0},{3,1},{4,6},{5,7},{6,4},{7,5},{8,10},{9,11},{10,... | collective-permute-start | bytes 786440 | tf_op jit(solution)/shard_map/ppermute | solution.py:421
  91.2 13.8 %collective-permute-start.2 = (bf16[1024,128]{1,0:T(8,128)(2,1)S(1)}, bf16[1024,128]{1,0:T(8,128)(2,1)S(1)}, u32[]{:S(2)}, u32[]{:S(2)}) collective-permute-start(bf16[1024,128]{1,0:T(8,128)(2,1)S(1)} %pack_weights.1.refs_0_), channel_id=1, source_target_pairs={{0,1},{1,2},{2,3},{3,0},{4,5},{5,6},{6,7},{7,4},{8,9},{9,10},{10,1... | collective-permute-start | bytes 786440 | tf_op jit(solution)/shard_map/ppermute | solution.py:421

commit v4 on v3

--- a/solution.py
+++ b/solution.py
@@ -24,7 +24,7 @@
 
 
 def silu(v):
-    return v / (1.0 + jnp.exp(-v))
+    return 0.5 * v * (1.0 + jnp.tanh(0.5 * v))
 
 
 def vmem_spec():
@@ -44,25 +44,17 @@
 
 
 def gather_kernel(rows_ref, mirror_ref, out_ref):
-    step = 1024
-    lanes = lax.broadcasted_iota(jnp.int32, (step, F), 1)
-
-    @pl.loop(0, ROWS // step)
-    def _(k):
-        picks = []
-        for half in range(step // F):
-            line = mirror_ref[pl.ds(k * (step // F) + half, 1), :]
-            picks.append(jnp.broadcast_to(line, (F, F)).T)
-        pick = jnp.concatenate(picks, axis=0)
-        hot = jnp.concatenate(
-            [
-                jnp.where(pick == lanes + j * F, 1.0, 0.0).astype(jnp.bfloat16)
-                for j in range(ROWS // F)
-            ],
-            axis=1,
-        )
-        got = mm(hot, rows_ref[...])
-        out_ref[pl.ds(pl.multiple_of(k * step, step), step), :] = got.astype(jnp.bfloat16)
+    half = ROWS // 2
+    pick = jnp.concatenate(
+        [jnp.broadcast_to(mirror_ref[j : j + 1, :], (F, F)).T for j in range(ROWS // F)], axis=0
+    )
+    within = pick & (half - 1)
+    lanes = lax.broadcasted_iota(jnp.int32, (ROWS, F), 1)
+    hot = jnp.concatenate(
+        [jnp.where(within == lanes + j * F, 1.0, 0.0).astype(jnp.bfloat16) for j in range(half // F)], axis=1
+    )
+    got = mm(hot, jnp.concatenate([rows_ref[:half], rows_ref[half:]], axis=1))
+    out_ref[...] = jnp.where(pick >= half, got[:, F:], got[:, :F]).astype(jnp.bfloat16)
 
 
 def gather_rows(rows, mirror):
@@ -291,7 +283,7 @@
     out_ref[:, CAP * AW :, :] = jnp.full((OWNERS, HEAD, F), -1.0, jnp.bfloat16)
     line = lax.broadcasted_iota(jnp.int32, (HEAD, F), 0)
 
-    @pl.loop(0, GROUPS, unroll=4)
+    @pl.loop(0, GROUPS, unroll=16)
     def _(g):
         owner = owner_ref[g]
         rank = seen_ref[owner]

time: 147 us -> 145 us (0.986)
  Pallas kernels: 15.2 us -> 13.6 us
  transfers between devices with their start and end apart: 8 -> 8, of which waited for: 7 -> 7; matrix products, arithmetic and copies ran while one was open for 0% -> 0% of each run, Pallas kernels for 5% -> 4%
where the time goes in v4:
time: 145 us; the launch traced here: 144 us
  waiting for transfers between devices  54.9 us (38%)
  starting transfers between devices  43.1 us (30%)
  blocking collectives  31.4 us (22%)
  Pallas kernels  13.6 us (9%)
    all_to_all x3, blocking collectives, transpose_mp(): return lax.all_to_all(x, 'mp', split_axis=0, concat_axis=0, tiled=True)  31.4 us
    all_to_all x2, waiting for transfers between devices, transpose_mp(): return lax.all_to_all(x, 'mp', split_axis=0, concat_axis=0, tiled=True)  23 us
    all_to_all x1, waiting for transfers between devices, body(): got = lax.all_to_all(sent, 'edge', split_axis=0, concat_axis=0, tiled=True)  16 us
    all_to_all x1, starting transfers between devices, body(): got = lax.all_to_all(sent, 'edge', split_axis=0, concat_axis=0, tiled=True)  12.2 us
    ppermute x3, waiting for transfers between devices, body(): lax.ppermute(atom_pack, 'mp', [(m, (m + shift) % MP) for m in range(MP)])  11.8 us
    ppermute x1, starting transfers between devices, body(): lax.ppermute(edge_feat, 'edge', [(e, e ^ half) for e in range(OWNERS)])  11.6 us
    ppermute x3, starting transfers between devices, body(): lax.ppermute(atom_pack, 'mp', [(m, (m + shift) % MP) for m in range(MP)])  7.81 us
    all_to_all x2, starting transfers between devices, transpose_mp(): return lax.all_to_all(x, 'mp', split_axis=0, concat_axis=0, tiled=True)  7.51 us
  transfers between devices with their start and end apart: 8, of which 7 were waited for; matrix products, arithmetic and copies ran while one was open for 0% of the time, Pallas kernels for 4%

profile of v4, /device:TPU:1, one launch (start us, length us, event | category | flops | bytes accessed | tf_op | source)
XLA Modules:
  0.0 144.1 jit_solution(10328321040401767138)
XLA Ops:
  0.0 0.0 copy-start
  0.0 11.6 %collective-permute-start = (bf16[2048,128]{1,0:T(8,128)(2,1)}, bf16[2048,128]{1,0:T(8,128)(2,1)S(1)}, u32[]{:S(2)}, u32[]{:S(2)}) collective-permute-start(bf16[2048,128]{1,0:T(8,128)(2,1)} %param.12), channel_id=1, source_target_pairs={{0,256},{4,260},{8,264},{12,268},{16,272},{20,276},{24,280},{28,28... | collective-permute-start | bytes 1572872 | tf_op jit(solution)/shard_map/ppermute | solution.py:397
  11.6 2.9 %share_rows_and_weights.1 = bf16[4,1536,128]{2,1,0:T(8,128)(2,1)} custom-call(bf16[4,512,128]{2,1,0:T(8,128)(2,1)} %bitcast.14, bf16[512,128]{1,0:T(8,128)(2,1)} %up_ref.1, bf16[128,512]{1,0:T(8,128)(2,1)} %down_ref.1, bf16[512,128]{1,0:T(8,128)(2,1)} %self_ref.1, bf16[512,128]{1,0:T(8,128)(2,1)} %mirror_ref.1), custom_call_target="tpu_custom_call" | custom-call | tf_op jit(solution)/shard_map/share_rows_and_weights/pallas_call | solution.py:172
  14.6 0.0 copy-start.6
  14.6 4.0 %all-to-all-start = ((bf16[4,1536,128]{2,1,0:T(8,128)(2,1)}), bf16[4,1536,128]{2,1,0:T(8,128)(2,1)S(1)}, u32[]{:S(2)}, u32[]{:S(2)}) async-start(bf16[4,1536,128]{2,1,0:T(8,128)(2,1)} %share_rows_and_weights.1), calls=%async_computation | async-start | bytes 3145728 | tf_op jit(solution)/shard_map/all_to_all | solution.py:379
  18.6 4.0 %collective-permute-done.rows_ref = bf16[2048,128]{1,0:T(8,128)(2,1)S(1)} collective-permute-done((bf16[2048,128]{1,0:T(8,128)(2,1)}, bf16[2048,128]{1,0:T(8,128)(2,1)S(1)}, u32[]{:S(2)}, u32[]{:S(2)}) %collective-permute-start) | collective-permute-done | bytes 524320 | tf_op jit(solution)/shard_map/ppermute | solution.py:397
  22.6 0.0 copy-done.6
  22.6 2.1 %gather_rows.1 = bf16[2048,128]{1,0:T(8,128)(2,1)} custom-call(bf16[2048,128]{1,0:T(8,128)(2,1)S(1)} %collective-permute-done.rows_ref, s32[16,128]{1,0:T(8,128)S(1)} %bitcast.12), custom_call_target="tpu_custom_call" | custom-call | flops 20000000000 | bytes 64000000 | tf_op jit(solution)/shard_map/gather_rows/pallas_call | solution.py:61
  24.8 13.4 %all-to-all-done.mine_ref = bf16[4,1536,128]{2,1,0:T(8,128)(2,1)S(1)} async-done(((bf16[4,1536,128]{2,1,0:T(8,128)(2,1)}), bf16[4,1536,128]{2,1,0:T(8,128)(2,1)S(1)}, u32[]{:S(2)}, u32[]{:S(2)}) %all-to-all-start) | async-done | bytes 1572896 | tf_op jit(solution)/shard_map/all_to_all | solution.py:379
  38.2 4.0 %collective-permute-start.1 = (bf16[4,1536,128]{2,1,0:T(8,128)(2,1)S(1)}, bf16[4,1536,128]{2,1,0:T(8,128)(2,1)}, u32[]{:S(2)}, u32[]{:S(2)}) collective-permute-start(bf16[4,1536,128]{2,1,0:T(8,128)(2,1)S(1)} %all-to-all-done.mine_ref), channel_id=1, source_target_pairs={{0,4},{4,0},{8,12},{12,8},{16,20},{20,16},{24,28},{28,24},{32,36},... | collective-permute-start | bytes 4718600 | tf_op jit(solution)/shard_map/ppermute | solution.py:403
  42.2 3.5 %all-to-all-start.1 = ((bf16[4,512,128]{2,1,0:T(8,128)(2,1)}), bf16[4,512,128]{2,1,0:T(8,128)(2,1)S(1)}, u32[]{:S(2)}, u32[]{:S(2)}) async-start(bf16[4,512,128]{2,1,0:T(8,128)(2,1)} %bitcast.3), calls=%async_computation.1 | async-start | bytes 1048576 | tf_op jit(solution)/shard_map/all_to_all | solution.py:379
  45.7 9.6 %all-to-all-done.1.rev_ref = bf16[4,512,128]{2,1,0:T(8,128)(2,1)S(1)} async-done(((bf16[4,512,128]{2,1,0:T(8,128)(2,1)}), bf16[4,512,128]{2,1,0:T(8,128)(2,1)S(1)}, u32[]{:S(2)}, u32[]{:S(2)}) %all-to-all-start.1) | async-done | bytes 524320 | tf_op jit(solution)/shard_map/all_to_all | solution.py:379
  55.3 0.0 collective-permute-done.1.other_hbm
  55.3 4.1 %edge_stage.1 = bf16[4,256,128]{2,1,0:T(8,128)(2,1)S(1)} custom-call(bf16[4,1536,128]{2,1,0:T(8,128)(2,1)S(1)} %all-to-all-done.mine_ref, bf16[4,1536,128]{2,1,0:T(8,128)(2,1)} %collective-permute-done.1.other_hbm, bf16[4,512,128]{2,1,0:T(8,128)(2,1)S(1)} %all-to-all-done.1.rev_ref, s32[1,512]{1,0:T(1,128)S(1)} %bitcast.9), custom_call_target="tpu_custom_call" | custom-call | tf_op jit(solution)/shard_map/edge_stage/pallas_call | solution.py:266
  59.4 9.4 %all_to_all.30 = bf16[4,256,128]{2,1,0:T(8,128)(2,1)S(1)} all-to-all(bf16[4,256,128]{2,1,0:T(8,128)(2,1)S(1)} %edge_stage.1), channel_id=1, replica_groups=mesh['edge'=128,'mp'=4] {'mp'}, dimensions={0} | all-to-all | bytes 524288 | tf_op jit(solution)/shard_map/all_to_all | solution.py:379
  68.8 2.4 %place_groups.1 = bf16[128,40,128]{2,1,0:T(8,128)(2,1)} custom-call(s32[64]{0:T(128)S(1)} %bitcast.11, s32[64]{0:T(128)S(1)} %copy-done.5, bf16[64,16,128]{2,1,0:T(8,128)(2,1)S(1)} %bitcast.8), custom_call_target="tpu_custom_call" | custom-call | tf_op jit(solution)/shard_map/place_groups/pallas_call | solution.py:298
  71.2 12.2 %all-to-all-start.3 = ((bf16[128,40,128]{2,1,0:T(8,128)(2,1)}), bf16[128,40,128]{2,1,0:T(8,128)(2,1)S(1)}, u32[]{:S(2)}, u32[]{:S(2)}) async-start(bf16[128,40,128]{2,1,0:T(8,128)(2,1)} %place_groups.1), calls=%async_computation.3 | async-start | bytes 2621440 | tf_op jit(solution)/shard_map/all_to_all | solution.py:415
  83.5 0.0 copy-done.1
  83.5 0.3 pack_weights.1.refs_0_
  83.8 0.0 copy-start.3
  83.8 2.8 %collective-permute-start.4 = (bf16[1024,128]{1,0:T(8,128)(2,1)S(1)}, bf16[1024,128]{1,0:T(8,128)(2,1)S(1)}, u32[]{:S(2)}, u32[]{:S(2)}) collective-permute-start(bf16[1024,128]{1,0:T(8,128)(2,1)S(1)} %pack_weights.1.refs_0_), channel_id=1, source_target_pairs={{0,3},{1,0},{2,1},{3,2},{4,7},{5,4},{6,5},{7,6},{8,11},{9,8},{10,9... | collective-permute-start | bytes 786440 | tf_op jit(solution)/shard_map/ppermute | solution.py:413
  86.6 3.1 %collective-permute-start.3 = (bf16[1024,128]{1,0:T(8,128)(2,1)S(1)}, bf16[1024,128]{1,0:T(8,128)(2,1)S(1)}, u32[]{:S(2)}, u32[]{:S(2)}) collective-permute-start(bf16[1024,128]{1,0:T(8,128)(2,1)S(1)} %pack_weights.1.refs_0_), channel_id=1, source_target_pairs={{0,2},{1,3},{2,0},{3,1},{4,6},{5,7},{6,4},{7,5},{8,10},{9,11},{10,... | collective-permute-start | bytes 786440 | tf_op jit(solution)/shard_map/ppermute | solution.py:413
  89.7 1.9 %collective-permute-start.2 = (bf16[1024,128]{1,0:T(8,128)(2,1)S(1)}, bf16[1024,128]{1,0:T(8,128)(2,1)S(1)}, u32[]{:S(2)}, u32[]{:S(2)}) collective-permute-start(bf16[1024,128]{1,0:T(8,128)(2,1)S(1)} %pack_weights.1.refs_0_), channel_id=1, source_target_pairs={{0,1},{1,2},{2,3},{3,0},{4,5},{5,6},{6,7},{7,4},{8,9},{9,10},{10,1... | collective-permute-start | bytes 786440 | tf_op jit(solution)/shard_map/ppermute | solution.py:413
  91.6 1.0 collective-permute-done.4.refs_3_
  92.6 4.0 %collective-permute-done.3.refs_2_ = bf16[1024,128]{1,0:T(8,128)(2,1)S(1)} collective-permute-done((bf16[1024,128]{1,0:T(8,128)(2,1)S(1)}, bf16[1024,128]{1,0:T(8,128)(2,1)S(1)}, u32[]{:S(2)}, u32[]{:S(2)}) %collective-permute-start.3) | collective-permute-done | bytes 262176 | tf_op jit(solution)/shard_map/ppermute | solution.py:413
  96.6 6.8 %collective-permute-done.2.refs_1_ = bf16[1024,128]{1,0:T(8,128)(2,1)S(1)} collective-permute-done((bf16[1024,128]{1,0:T(8,128)(2,1)S(1)}, bf16[1024,128]{1,0:T(8,128)(2,1)S(1)}, u32[]{:S(2)}, u32[]{:S(2)}) %collective-permute-start.2) | collective-permute-done | bytes 262176 | tf_op jit(solution)/shard_map/ppermute | solution.py:413
  103.5 16.0 %all-to-all-done.3.got_ref = bf16[128,40,128]{2,1,0:T(8,128)(2,1)S(1)} async-done(((bf16[128,40,128]{2,1,0:T(8,128)(2,1)}), bf16[128,40,128]{2,1,0:T(8,128)(2,1)S(1)}, u32[]{:S(2)}, u32[]{:S(2)}) %all-to-all-start.3) | async-done | bytes 1310752 | tf_op jit(solution)/shard_map/all_to_all | solution.py:415
  119.5 0.9 collect_blocks.1
  120.4 11.6 %all_to_all.31.x_ref = bf16[4,512,128]{2,1,0:T(8,128)(2,1)S(1)} all-to-all(bf16[4,512,128]{2,1,0:T(8,128)(2,1)S(1)} %collect_blocks.1), channel_id=1, replica_groups=mesh['edge'=128,'mp'=4] {'mp'}, dimensions={0} | all-to-all | bytes 1048576 | tf_op jit(solution)/shard_map/all_to_all | solution.py:379
  132.0 0.9 atom_stage.1
  132.9 10.4 %all_to_all.32 = bf16[4,512,128]{2,1,0:T(8,128)(2,1)S(1)} all-to-all(bf16[4,512,128]{2,1,0:T(8,128)(2,1)S(1)} %atom_stage.1), channel_id=1, replica_groups=mesh['edge'=128,'mp'=4] {'mp'}, dimensions={0} | all-to-all | bytes 1048576 | tf_op jit(solution)/shard_map/all_to_all | solution.py:379
  143.3 0.8 copy.14
  (10 shorter events, 0.0 us)
Async XLA Ops:
  0.0 45.7 %copy-start = (s32[16,128]{1,0:T(8,128)S(1)}, s32[16,128]{1,0:T(8,128)}, u32[]{:S(2)}) copy-start(s32[16,128]{1,0:T(8,128)} %param.14) | copy-start | bytes 24580
  0.0 22.6 %collective-permute-start = (bf16[2048,128]{1,0:T(8,128)(2,1)}, bf16[2048,128]{1,0:T(8,128)(2,1)S(1)}, u32[]{:S(2)}, u32[]{:S(2)}) collective-permute-start(bf16[2048,128]{1,0:T(8,128)(2,1)} %param.12), channel_id=1, source_target_pairs={{0,256},{4,260},{8,264},{12,268},{16,272},{20,276},{24,280},{28,28... | collective-permute-start | bytes 1572872 | tf_op jit(solution)/shard_map/ppermute | solution.py:397
  14.6 8.1 %copy-start.6 = (s32[2048]{0:T(1024)S(1)}, s32[2048]{0:T(1024)}, u32[]{:S(2)}) copy-start(s32[2048]{0:T(1024)} %param.13) | copy-start | bytes 24580
  14.6 23.6 %all-to-all-start = ((bf16[4,1536,128]{2,1,0:T(8,128)(2,1)}), bf16[4,1536,128]{2,1,0:T(8,128)(2,1)S(1)}, u32[]{:S(2)}, u32[]{:S(2)}) async-start(bf16[4,1536,128]{2,1,0:T(8,128)(2,1)} %share_rows_and_weights.1), calls=%async_computation | async-start | bytes 3145728 | tf_op jit(solution)/shard_map/all_to_all | solution.py:379
  38.2 17.1 %collective-permute-start.1 = (bf16[4,1536,128]{2,1,0:T(8,128)(2,1)S(1)}, bf16[4,1536,128]{2,1,0:T(8,128)(2,1)}, u32[]{:S(2)}, u32[]{:S(2)}) collective-permute-start(bf16[4,1536,128]{2,1,0:T(8,128)(2,1)S(1)} %all-to-all-done.mine_ref), channel_id=1, source_target_pairs={{0,4},{4,0},{8,12},{12,8},{16,20},{20,16},{24,28},{28,24},{32,36},... | collective-permute-start | bytes 4718600 | tf_op jit(solution)/shard_map/ppermute | solution.py:403
  42.2 13.1 %all-to-all-start.1 = ((bf16[4,512,128]{2,1,0:T(8,128)(2,1)}), bf16[4,512,128]{2,1,0:T(8,128)(2,1)S(1)}, u32[]{:S(2)}, u32[]{:S(2)}) async-start(bf16[4,512,128]{2,1,0:T(8,128)(2,1)} %bitcast.3), calls=%async_computation.1 | async-start | bytes 1048576 | tf_op jit(solution)/shard_map/all_to_all | solution.py:379
  55.3 13.6 %copy-start.4 = (s32[64,1]{0,1:T(1,128)S(1)}, s32[64,1]{0,1:T(1,128)}, u32[]{:S(2)}) copy-start(s32[64,1]{0,1:T(1,128)} %param.15) | copy-start | bytes 772
  55.3 13.6 %copy-start.5 = (s32[64]{0:T(128)S(1)}, s32[64]{0:T(128)}, u32[]{:S(2)}) copy-start(s32[64]{0:T(128)} %window_ref.1) | copy-start | bytes 772
  71.2 12.2 %copy-start.1 = (bf16[512,128]{1,0:T(8,128)(2,1)S(1)}, bf16[512,128]{1,0:T(8,128)(2,1)}, u32[]{:S(2)}) copy-start(bf16[512,128]{1,0:T(8,128)(2,1)} %refs_0_) | copy-start | bytes 393220
  71.2 12.3 %copy-start.2 = (bf16[128,512]{1,0:T(8,128)(2,1)S(1)}, bf16[128,512]{1,0:T(8,128)(2,1)}, u32[]{:S(2)}) copy-start(bf16[128,512]{1,0:T(8,128)(2,1)} %refs_1_) | copy-start | bytes 393220
  71.2 48.3 %all-to-all-start.3 = ((bf16[128,40,128]{2,1,0:T(8,128)(2,1)}), bf16[128,40,128]{2,1,0:T(8,128)(2,1)S(1)}, u32[]{:S(2)}, u32[]{:S(2)}) async-start(bf16[128,40,128]{2,1,0:T(8,128)(2,1)} %place_groups.1), calls=%async_computation.3 | async-start | bytes 2621440 | tf_op jit(solution)/shard_map/all_to_all | solution.py:415
  83.8 48.2 %copy-start.3 = (f32[512]{0:T(512)S(1)}, f32[512]{0:T(512)}, u32[]{:S(2)}) copy-start(f32[512]{0:T(512)} %param.23) | copy-start | bytes 6148
  83.8 8.8 %collective-permute-start.4 = (bf16[1024,128]{1,0:T(8,128)(2,1)S(1)}, bf16[1024,128]{1,0:T(8,128)(2,1)S(1)}, u32[]{:S(2)}, u32[]{:S(2)}) collective-permute-start(bf16[1024,128]{1,0:T(8,128)(2,1)S(1)} %pack_weights.1.refs_0_), channel_id=1, source_target_pairs={{0,3},{1,0},{2,1},{3,2},{4,7},{5,4},{6,5},{7,6},{8,11},{9,8},{10,9... | collective-permute-start | bytes 786440 | tf_op jit(solution)/shard_map/ppermute | solution.py:413
  86.6 10.0 %collective-permute-start.3 = (bf16[1024,128]{1,0:T(8,128)(2,1)S(1)}, bf16[1024,128]{1,0:T(8,128)(2,1)S(1)}, u32[]{:S(2)}, u32[]{:S(2)}) collective-permute-start(bf16[1024,128]{1,0:T(8,128)(2,1)S(1)} %pack_weights.1.refs_0_), channel_id=1, source_target_pairs={{0,2},{1,3},{2,0},{3,1},{4,6},{5,7},{6,4},{7,5},{8,10},{9,11},{10,... | collective-permute-start | bytes 786440 | tf_op jit(solution)/shard_map/ppermute | solution.py:413
  89.7 13.8 %collective-permute-start.2 = (bf16[1024,128]{1,0:T(8,128)(2,1)S(1)}, bf16[1024,128]{1,0:T(8,128)(2,1)S(1)}, u32[]{:S(2)}, u32[]{:S(2)}) collective-permute-start(bf16[1024,128]{1,0:T(8,128)(2,1)S(1)} %pack_weights.1.refs_0_), channel_id=1, source_target_pairs={{0,1},{1,2},{2,3},{3,0},{4,5},{5,6},{6,7},{7,4},{8,9},{9,10},{10,1... | collective-permute-start | bytes 786440 | tf_op jit(solution)/shard_map/ppermute | solution.py:413

commit v5 on v4

--- a/solution.py
+++ b/solution.py
@@ -97,6 +97,22 @@
         compiler_params=params(),
         name="send_windows",
     )(owner.reshape(1, GROUPS), window.reshape(1, GROUPS))
+
+
+def after_kernel(slot_ref, rows_ref, out_ref):
+    out_ref[...] = slot_ref[...]
+
+
+def after_rows(slots, rows):
+    return pl.pallas_call(
+        after_kernel,
+        out_shape=jax.ShapeDtypeStruct(slots.shape, slots.dtype),
+        in_specs=[vmem_spec(), pl.BlockSpec(memory_space=pl.ANY)],
+        out_specs=vmem_spec(),
+        compiler_params=params(),
+        cost_estimate=pl.CostEstimate(flops=40_000_000_000, bytes_accessed=128_000_000, transcendentals=0),
+        name="after_rows",
+    )(slots, rows)
 
 
 def pack_kernel(*refs):
@@ -400,11 +416,12 @@
         share(edge_feat.reshape(MP, OWN, F), up_edge, down_edge, mix_self, mix_mirror)
     )
     reverse, mine = lax.optimization_barrier((gather_rows(partner, mirror_rows), mine))
-    other = lax.ppermute(mine, "edge", [(e, e ^ 1) for e in range(OWNERS)])
     rev = transpose_mp(reverse.reshape(MP, OWN, F))
     me = lax.axis_index("mp")
-    slots = lax.dynamic_slice(edge_slot, (me * (OWN // F), 0), (OWN // F, F)).reshape(1, OWN)
-    partial = edge_stage(mine, other, rev, slots)
+    slots = lax.dynamic_slice(edge_slot, (me * (OWN // F), 0), (OWN // F, F))
+    slots, mine = lax.optimization_barrier((after_rows(slots, reverse), mine))
+    other = lax.ppermute(mine, "edge", [(e, e ^ 1) for e in range(OWNERS)])
+    partial = edge_stage(mine, other, rev, slots.reshape(1, OWN))
     blocks = transpose_mp(partial).reshape(GROUPS, AW, F)
     sent = place(owner, group_window, blocks)
     sent, up_atom, down_atom = lax.optimization_barrier((sent, up_atom, down_atom))

time: 145 us -> 143 us (0.986)
  blocking collectives: 31.4 us -> 41.7 us
  waiting for transfers between devices: 54.9 us -> 46.1 us
  Pallas kernels: 13.6 us -> 10.8 us
  starting transfers between devices: 43.1 us -> 41.6 us
    all_to_all x3 -> x4, blocking collectives: 31.4 us -> 41.7 us  [transpose_mp(): return lax.all_to_all(x, 'mp', split_axis=0, concat_axis=0, tiled=True)]
    all_to_all x2 -> x1, waiting for transfers between devices: 23 us -> 14.2 us  [transpose_mp(): return lax.all_to_all(x, 'mp', split_axis=0, concat_axis=0, tiled=True)]
    all_to_all x2 -> x1, starting transfers between devices: 7.51 us -> 4.02 us  [transpose_mp(): return lax.all_to_all(x, 'mp', split_axis=0, concat_axis=0, tiled=True)]
    all_to_all x1, starting transfers between devices: 12.2 us -> 14.2 us  [body(): got = lax.all_to_all(sent, 'edge', split_axis=0, concat_axis=0, tiled=True)]
  transfers between devices with their start and end apart: 8 -> 7, of which waited for: 7 -> 6; matrix products, arithmetic and copies ran while one was open for 0% -> 0% of each run, Pallas kernels for 4% -> 3%
where the time goes in v5:
time: 143 us; the launch traced here: 142 us
  waiting for transfers between devices  46.1 us (32%)
  blocking collectives  41.7 us (29%)
  starting transfers between devices  41.6 us (29%)
  Pallas kernels  10.8 us (8%)
  local copies, waits for them, and re-layouts  1.89 us (1%)
    all_to_all x4, blocking collectives, transpose_mp(): return lax.all_to_all(x, 'mp', split_axis=0, concat_axis=0, tiled=True)  41.7 us
    all_to_all x1, waiting for transfers between devices, body(): got = lax.all_to_all(sent, 'edge', split_axis=0, concat_axis=0, tiled=True)  16 us
    all_to_all x1, waiting for transfers between devices, transpose_mp(): return lax.all_to_all(x, 'mp', split_axis=0, concat_axis=0, tiled=True)  14.2 us
    all_to_all x1, starting transfers between devices, body(): got = lax.all_to_all(sent, 'edge', split_axis=0, concat_axis=0, tiled=True)  14.2 us
    ppermute x3, waiting for transfers between devices, body(): lax.ppermute(atom_pack, 'mp', [(m, (m + shift) % MP) for m in range(MP)])  11.8 us
    ppermute x1, starting transfers between devices, body(): lax.ppermute(edge_feat, 'edge', [(e, e ^ half) for e in range(OWNERS)])  11.6 us
    ppermute x3, starting transfers between devices, body(): lax.ppermute(atom_pack, 'mp', [(m, (m + shift) % MP) for m in range(MP)])  7.81 us
    ppermute x1, waiting for transfers between devices, body(): lax.ppermute(edge_feat, 'edge', [(e, e ^ half) for e in range(OWNERS)])  4.03 us
  transfers between devices with their start and end apart: 7, of which 6 were waited for; matrix products, arithmetic and copies ran while one was open for 0% of the time, Pallas kernels for 3%

profile of v5, /device:TPU:1, one launch (start us, length us, event | category | flops | bytes accessed | tf_op | source)
XLA Modules:
  0.0 142.2 jit_solution(9630423684968963469)
XLA Ops:
  0.0 0.0 copy-start
  0.0 11.6 %collective-permute-start = (bf16[2048,128]{1,0:T(8,128)(2,1)}, bf16[2048,128]{1,0:T(8,128)(2,1)S(1)}, u32[]{:S(2)}, u32[]{:S(2)}) collective-permute-start(bf16[2048,128]{1,0:T(8,128)(2,1)} %param.12), channel_id=1, source_target_pairs={{0,256},{4,260},{8,264},{12,268},{16,272},{20,276},{24,280},{28,28... | collective-permute-start | bytes 1572872 | tf_op jit(solution)/shard_map/ppermute | solution.py:413
  11.6 3.0 %share_rows_and_weights.1 = bf16[4,1536,128]{2,1,0:T(8,128)(2,1)} custom-call(bf16[4,512,128]{2,1,0:T(8,128)(2,1)} %bitcast.15, bf16[512,128]{1,0:T(8,128)(2,1)} %up_ref.1, bf16[128,512]{1,0:T(8,128)(2,1)} %down_ref.1, bf16[512,128]{1,0:T(8,128)(2,1)} %self_ref.1, bf16[512,128]{1,0:T(8,128)(2,1)} %mirror_ref.1), custom_call_target="tpu_custom_call" | custom-call | tf_op jit(solution)/shard_map/share_rows_and_weights/pallas_call | solution.py:188
  14.6 0.0 copy-start.7
  14.6 4.0 %all-to-all-start = ((bf16[4,1536,128]{2,1,0:T(8,128)(2,1)}), bf16[4,1536,128]{2,1,0:T(8,128)(2,1)S(1)}, u32[]{:S(2)}, u32[]{:S(2)}) async-start(bf16[4,1536,128]{2,1,0:T(8,128)(2,1)} %share_rows_and_weights.1), calls=%async_computation | async-start | bytes 3145728 | tf_op jit(solution)/shard_map/all_to_all | solution.py:395
  18.6 0.0 copy-done
  18.6 4.0 %collective-permute-done.rows_ref = bf16[2048,128]{1,0:T(8,128)(2,1)S(1)} collective-permute-done((bf16[2048,128]{1,0:T(8,128)(2,1)}, bf16[2048,128]{1,0:T(8,128)(2,1)S(1)}, u32[]{:S(2)}, u32[]{:S(2)}) %collective-permute-start) | collective-permute-done | bytes 524320 | tf_op jit(solution)/shard_map/ppermute | solution.py:413
  22.6 0.0 copy-done.7
  22.6 1.3 gather_rows.1.rows_ref
  24.0 14.2 %all-to-all-done.mine_ref = bf16[4,1536,128]{2,1,0:T(8,128)(2,1)S(1)} async-done(((bf16[4,1536,128]{2,1,0:T(8,128)(2,1)}), bf16[4,1536,128]{2,1,0:T(8,128)(2,1)S(1)}, u32[]{:S(2)}, u32[]{:S(2)}) %all-to-all-start) | async-done | bytes 1572896 | tf_op jit(solution)/shard_map/all_to_all | solution.py:395
  38.2 4.0 %collective-permute-start.1 = (bf16[4,1536,128]{2,1,0:T(8,128)(2,1)S(1)}, bf16[4,1536,128]{2,1,0:T(8,128)(2,1)S(1)}, u32[]{:S(2)}, u32[]{:S(2)}) collective-permute-start(bf16[4,1536,128]{2,1,0:T(8,128)(2,1)S(1)} %all-to-all-done.mine_ref), channel_id=1, source_target_pairs={{0,4},{4,0},{8,12},{12,8},{16,20},{20,16},{24,28},{28,24},{32,36},... | collective-permute-start | bytes 4718600 | tf_op jit(solution)/shard_map/ppermute | solution.py:423
  42.2 11.7 %all_to_all.30.rev_ref = bf16[4,512,128]{2,1,0:T(8,128)(2,1)S(1)} all-to-all(bf16[4,512,128]{2,1,0:T(8,128)(2,1)S(1)} %bitcast.9), channel_id=1, replica_groups=mesh['edge'=128,'mp'=4] {'mp'}, dimensions={0} | all-to-all | bytes 1048576 | tf_op jit(solution)/shard_map/all_to_all | solution.py:395
  53.9 0.0 collective-permute-done.1.other_hbm
  53.9 3.2 %edge_stage.1 = bf16[4,256,128]{2,1,0:T(8,128)(2,1)S(1)} custom-call(bf16[4,1536,128]{2,1,0:T(8,128)(2,1)S(1)} %all-to-all-done.mine_ref, bf16[4,1536,128]{2,1,0:T(8,128)(2,1)S(1)} %collective-permute-done.1.other_hbm, bf16[4,512,128]{2,1,0:T(8,128)(2,1)S(1)} %all_to_all.30.rev_ref, s32[1,512]{1,0:T(1,128)S(1)} %bitcast.10), custom_call_target="tpu_custom_call" | custom-call | tf_op jit(solution)/shard_map/edge_stage/pallas_call | solution.py:282
  57.1 7.9 %all_to_all.31 = bf16[4,256,128]{2,1,0:T(8,128)(2,1)S(1)} all-to-all(bf16[4,256,128]{2,1,0:T(8,128)(2,1)S(1)} %edge_stage.1), channel_id=1, replica_groups=mesh['edge'=128,'mp'=4] {'mp'}, dimensions={0} | all-to-all | bytes 524288 | tf_op jit(solution)/shard_map/all_to_all | solution.py:395
  65.1 1.3 place_groups.1
  66.4 1.1 copy-done.1
  67.4 14.2 %all-to-all-start.3 = ((bf16[128,40,128]{2,1,0:T(8,128)(2,1)}), bf16[128,40,128]{2,1,0:T(8,128)(2,1)S(1)}, u32[]{:S(2)}, u32[]{:S(2)}) async-start(bf16[128,40,128]{2,1,0:T(8,128)(2,1)} %copy-done.1), calls=%async_computation.3 | async-start | bytes 2621440 | tf_op jit(solution)/shard_map/all_to_all | solution.py:432
  81.6 0.3 pack_weights.1.refs_0_
  81.9 0.0 copy-start.4
  82.0 2.8 %collective-permute-start.4 = (bf16[1024,128]{1,0:T(8,128)(2,1)S(1)}, bf16[1024,128]{1,0:T(8,128)(2,1)S(1)}, u32[]{:S(2)}, u32[]{:S(2)}) collective-permute-start(bf16[1024,128]{1,0:T(8,128)(2,1)S(1)} %pack_weights.1.refs_0_), channel_id=1, source_target_pairs={{0,3},{1,0},{2,1},{3,2},{4,7},{5,4},{6,5},{7,6},{8,11},{9,8},{10,9... | collective-permute-start | bytes 786440 | tf_op jit(solution)/shard_map/ppermute | solution.py:430
  84.8 3.1 %collective-permute-start.3 = (bf16[1024,128]{1,0:T(8,128)(2,1)S(1)}, bf16[1024,128]{1,0:T(8,128)(2,1)S(1)}, u32[]{:S(2)}, u32[]{:S(2)}) collective-permute-start(bf16[1024,128]{1,0:T(8,128)(2,1)S(1)} %pack_weights.1.refs_0_), channel_id=1, source_target_pairs={{0,2},{1,3},{2,0},{3,1},{4,6},{5,7},{6,4},{7,5},{8,10},{9,11},{10,... | collective-permute-start | bytes 786440 | tf_op jit(solution)/shard_map/ppermute | solution.py:430
  87.9 1.9 %collective-permute-start.2 = (bf16[1024,128]{1,0:T(8,128)(2,1)S(1)}, bf16[1024,128]{1,0:T(8,128)(2,1)S(1)}, u32[]{:S(2)}, u32[]{:S(2)}) collective-permute-start(bf16[1024,128]{1,0:T(8,128)(2,1)S(1)} %pack_weights.1.refs_0_), channel_id=1, source_target_pairs={{0,1},{1,2},{2,3},{3,0},{4,5},{5,6},{6,7},{7,4},{8,9},{9,10},{10,1... | collective-permute-start | bytes 786440 | tf_op jit(solution)/shard_map/ppermute | solution.py:430
  89.8 1.0 collective-permute-done.4.refs_3_
  90.8 4.0 %collective-permute-done.3.refs_2_ = bf16[1024,128]{1,0:T(8,128)(2,1)S(1)} collective-permute-done((bf16[1024,128]{1,0:T(8,128)(2,1)S(1)}, bf16[1024,128]{1,0:T(8,128)(2,1)S(1)}, u32[]{:S(2)}, u32[]{:S(2)}) %collective-permute-start.3) | collective-permute-done | bytes 262176 | tf_op jit(solution)/shard_map/ppermute | solution.py:430
  94.8 6.8 %collective-permute-done.2.refs_1_ = bf16[1024,128]{1,0:T(8,128)(2,1)S(1)} collective-permute-done((bf16[1024,128]{1,0:T(8,128)(2,1)S(1)}, bf16[1024,128]{1,0:T(8,128)(2,1)S(1)}, u32[]{:S(2)}, u32[]{:S(2)}) %collective-permute-start.2) | collective-permute-done | bytes 262176 | tf_op jit(solution)/shard_map/ppermute | solution.py:430
  101.6 16.0 %all-to-all-done.3.got_ref = bf16[128,40,128]{2,1,0:T(8,128)(2,1)S(1)} async-done(((bf16[128,40,128]{2,1,0:T(8,128)(2,1)}), bf16[128,40,128]{2,1,0:T(8,128)(2,1)S(1)}, u32[]{:S(2)}, u32[]{:S(2)}) %all-to-all-start.3) | async-done | bytes 1310752 | tf_op jit(solution)/shard_map/all_to_all | solution.py:432
  117.7 0.9 collect_blocks.1
  118.6 11.6 %all_to_all.32.x_ref = bf16[4,512,128]{2,1,0:T(8,128)(2,1)S(1)} all-to-all(bf16[4,512,128]{2,1,0:T(8,128)(2,1)S(1)} %collect_blocks.1), channel_id=1, replica_groups=mesh['edge'=128,'mp'=4] {'mp'}, dimensions={0} | all-to-all | bytes 1048576 | tf_op jit(solution)/shard_map/all_to_all | solution.py:395
  130.2 0.9 atom_stage.1
  131.1 10.4 %all_to_all.33 = bf16[4,512,128]{2,1,0:T(8,128)(2,1)S(1)} all-to-all(bf16[4,512,128]{2,1,0:T(8,128)(2,1)S(1)} %atom_stage.1), channel_id=1, replica_groups=mesh['edge'=128,'mp'=4] {'mp'}, dimensions={0} | all-to-all | bytes 1048576 | tf_op jit(solution)/shard_map/all_to_all | solution.py:395
  141.5 0.8 copy.14
  (12 shorter events, 0.0 us)
Async XLA Ops:
  0.0 18.6 %copy-start = (s32[16,128]{1,0:T(8,128)S(1)}, s32[16,128]{1,0:T(8,128)}, u32[]{:S(2)}) copy-start(s32[16,128]{1,0:T(8,128)} %param.14) | copy-start | bytes 24580
  0.0 22.6 %collective-permute-start = (bf16[2048,128]{1,0:T(8,128)(2,1)}, bf16[2048,128]{1,0:T(8,128)(2,1)S(1)}, u32[]{:S(2)}, u32[]{:S(2)}) collective-permute-start(bf16[2048,128]{1,0:T(8,128)(2,1)} %param.12), channel_id=1, source_target_pairs={{0,256},{4,260},{8,264},{12,268},{16,272},{20,276},{24,280},{28,28... | collective-permute-start | bytes 1572872 | tf_op jit(solution)/shard_map/ppermute | solution.py:413
  14.6 8.1 %copy-start.7 = (s32[2048]{0:T(1024)S(1)}, s32[2048]{0:T(1024)}, u32[]{:S(2)}) copy-start(s32[2048]{0:T(1024)} %param.13) | copy-start | bytes 24580
  14.6 23.6 %all-to-all-start = ((bf16[4,1536,128]{2,1,0:T(8,128)(2,1)}), bf16[4,1536,128]{2,1,0:T(8,128)(2,1)S(1)}, u32[]{:S(2)}, u32[]{:S(2)}) async-start(bf16[4,1536,128]{2,1,0:T(8,128)(2,1)} %share_rows_and_weights.1), calls=%async_computation | async-start | bytes 3145728 | tf_op jit(solution)/shard_map/all_to_all | solution.py:395
  38.2 15.7 %collective-permute-start.1 = (bf16[4,1536,128]{2,1,0:T(8,128)(2,1)S(1)}, bf16[4,1536,128]{2,1,0:T(8,128)(2,1)S(1)}, u32[]{:S(2)}, u32[]{:S(2)}) collective-permute-start(bf16[4,1536,128]{2,1,0:T(8,128)(2,1)S(1)} %all-to-all-done.mine_ref), channel_id=1, source_target_pairs={{0,4},{4,0},{8,12},{12,8},{16,20},{20,16},{24,28},{28,24},{32,36},... | collective-permute-start | bytes 4718600 | tf_op jit(solution)/shard_map/ppermute | solution.py:423
  53.9 11.1 %copy-start.5 = (s32[64,1]{0,1:T(1,128)S(1)}, s32[64,1]{0,1:T(1,128)}, u32[]{:S(2)}) copy-start(s32[64,1]{0,1:T(1,128)} %param.15) | copy-start | bytes 772
  53.9 11.1 %copy-start.6 = (s32[64]{0:T(128)S(1)}, s32[64]{0:T(128)}, u32[]{:S(2)}) copy-start(s32[64]{0:T(128)} %window_ref.1) | copy-start | bytes 772
  66.4 1.1 copy-start.1
  67.4 14.2 %copy-start.2 = (bf16[512,128]{1,0:T(8,128)(2,1)S(1)}, bf16[512,128]{1,0:T(8,128)(2,1)}, u32[]{:S(2)}) copy-start(bf16[512,128]{1,0:T(8,128)(2,1)} %refs_0_) | copy-start | bytes 393220
  67.4 14.2 %copy-start.3 = (bf16[128,512]{1,0:T(8,128)(2,1)S(1)}, bf16[128,512]{1,0:T(8,128)(2,1)}, u32[]{:S(2)}) copy-start(bf16[128,512]{1,0:T(8,128)(2,1)} %refs_1_) | copy-start | bytes 393220
  67.4 50.2 %all-to-all-start.3 = ((bf16[128,40,128]{2,1,0:T(8,128)(2,1)}), bf16[128,40,128]{2,1,0:T(8,128)(2,1)S(1)}, u32[]{:S(2)}, u32[]{:S(2)}) async-start(bf16[128,40,128]{2,1,0:T(8,128)(2,1)} %copy-done.1), calls=%async_computation.3 | async-start | bytes 2621440 | tf_op jit(solution)/shard_map/all_to_all | solution.py:432
  81.9 48.2 %copy-start.4 = (f32[512]{0:T(512)S(1)}, f32[512]{0:T(512)}, u32[]{:S(2)}) copy-start(f32[512]{0:T(512)} %param.23) | copy-start | bytes 6148
  82.0 8.8 %collective-permute-start.4 = (bf16[1024,128]{1,0:T(8,128)(2,1)S(1)}, bf16[1024,128]{1,0:T(8,128)(2,1)S(1)}, u32[]{:S(2)}, u32[]{:S(2)}) collective-permute-start(bf16[1024,128]{1,0:T(8,128)(2,1)S(1)} %pack_weights.1.refs_0_), channel_id=1, source_target_pairs={{0,3},{1,0},{2,1},{3,2},{4,7},{5,4},{6,5},{7,6},{8,11},{9,8},{10,9... | collective-permute-start | bytes 786440 | tf_op jit(solution)/shard_map/ppermute | solution.py:430
  84.8 10.0 %collective-permute-start.3 = (bf16[1024,128]{1,0:T(8,128)(2,1)S(1)}, bf16[1024,128]{1,0:T(8,128)(2,1)S(1)}, u32[]{:S(2)}, u32[]{:S(2)}) collective-permute-start(bf16[1024,128]{1,0:T(8,128)(2,1)S(1)} %pack_weights.1.refs_0_), channel_id=1, source_target_pairs={{0,2},{1,3},{2,0},{3,1},{4,6},{5,7},{6,4},{7,5},{8,10},{9,11},{10,... | collective-permute-start | bytes 786440 | tf_op jit(solution)/shard_map/ppermute | solution.py:430
  87.9 13.8 %collective-permute-start.2 = (bf16[1024,128]{1,0:T(8,128)(2,1)S(1)}, bf16[1024,128]{1,0:T(8,128)(2,1)S(1)}, u32[]{:S(2)}, u32[]{:S(2)}) collective-permute-start(bf16[1024,128]{1,0:T(8,128)(2,1)S(1)} %pack_weights.1.refs_0_), channel_id=1, source_target_pairs={{0,1},{1,2},{2,3},{3,0},{4,5},{5,6},{6,7},{7,4},{8,9},{9,10},{10,1... | collective-permute-start | bytes 786440 | tf_op jit(solution)/shard_map/ppermute | solution.py:430

commit v6 on v5

--- a/solution.py
+++ b/solution.py
@@ -153,35 +153,35 @@
     return lax.rem(lax.axis_index("edge"), 2)
 
 
-def share_kernel(rows_ref, up_ref, down_ref, self_ref, mirror_ref, out_ref, held, sems):
-    def move(moves):
-        copies = [pltpu.make_async_copy(src, dst, sems.at[k]) for k, (src, dst) in enumerate(moves)]
-        for copy in copies:
+def share_kernel(rows_ref, up_ref, down_ref, self_ref, mirror_ref, out_ref, held, weights, sems):
+    def copies(moves, first):
+        made = [pltpu.make_async_copy(src, dst, sems.at[first + k]) for k, (src, dst) in enumerate(moves)]
+        for copy in made:
             copy.start()
-        for copy in copies:
+        return made
+
+    def wait(made):
+        for copy in made:
             copy.wait()
 
-    own = [(rows_ref, held.at[:, pl.ds(0, OWN)])]
+    rows_in = copies([(rows_ref, held)], 0)
     core = core_index()
 
     @pl.when(core == 0)
     def _():
-        moves = list(own)
-        for m in range(MP):
-            moves.append((up_ref, held.at[m, pl.ds(OWN, D)]))
-            for j in range(MP):
-                moves.append((down_ref.at[:, pl.ds(j * F, F)], held.at[m, pl.ds(OWN + D + j * F, F)]))
-        move(moves)
+        moves = [(up_ref, weights.at[pl.ds(0, D)])]
+        for j in range(MP):
+            moves.append((down_ref.at[:, pl.ds(j * F, F)], weights.at[pl.ds(D + j * F, F)]))
+        wait(copies(moves, 1))
 
     @pl.when(core != 0)
     def _():
-        moves = list(own)
-        for m in range(MP):
-            moves.append((self_ref, held.at[m, pl.ds(OWN, D)]))
-            moves.append((mirror_ref, held.at[m, pl.ds(OWN + D, D)]))
-        move(moves)
-
-    move([(held, out_ref)])
+        wait(copies([(self_ref, weights.at[pl.ds(0, D)]), (mirror_ref, weights.at[pl.ds(D, D)])], 1))
+
+    out = copies([(weights, out_ref.at[m, pl.ds(OWN, 2 * D)]) for m in range(MP)], 2 + MP)
+    wait(rows_in)
+    out += copies([(held, out_ref.at[:, pl.ds(0, OWN)])], 2 + 2 * MP)
+    wait(out)
 
 
 def share(rows, *weights):
@@ -191,8 +191,9 @@
         in_specs=[pl.BlockSpec(memory_space=pl.ANY)] * 5,
         out_specs=pl.BlockSpec(memory_space=pl.ANY),
         scratch_shapes=[
-            pltpu.VMEM((MP, PIECE, F), jnp.bfloat16),
-            pltpu.SemaphoreType.DMA((1 + MP * (1 + MP),)),
+            pltpu.VMEM((MP, OWN, F), jnp.bfloat16),
+            pltpu.VMEM((2 * D, F), jnp.bfloat16),
+            pltpu.SemaphoreType.DMA((3 + 2 * MP,)),
         ],
         compiler_params=pltpu.CompilerParams(vmem_limit_bytes=ALL_VMEM),
         name="share_rows_and_weights",

time: 143 us -> 143 us (level)
  no operation moved by 1% of the time
where the time goes in v6:
time: 143 us; the launch traced here: 142 us
  waiting for transfers between devices  46.1 us (32%)
  starting transfers between devices  42.2 us (30%)
  blocking collectives  41.7 us (29%)
  Pallas kernels  10.3 us (7%)
  local copies, waits for them, and re-layouts  1.89 us (1%)
    all_to_all x4, blocking collectives, transpose_mp(): return lax.all_to_all(x, 'mp', split_axis=0, concat_axis=0, tiled=True)  41.7 us
    all_to_all x1, waiting for transfers between devices, body(): got = lax.all_to_all(sent, 'edge', split_axis=0, concat_axis=0, tiled=True)  16 us
    all_to_all x1, starting transfers between devices, body(): got = lax.all_to_all(sent, 'edge', split_axis=0, concat_axis=0, tiled=True)  14.7 us
    all_to_all x1, waiting for transfers between devices, transpose_mp(): return lax.all_to_all(x, 'mp', split_axis=0, concat_axis=0, tiled=True)  13.6 us
    ppermute x3, waiting for transfers between devices, body(): lax.ppermute(atom_pack, 'mp', [(m, (m + shift) % MP) for m in range(MP)])  11.8 us
    ppermute x1, starting transfers between devices, body(): lax.ppermute(edge_feat, 'edge', [(e, e ^ half) for e in range(OWNERS)])  11.6 us
    ppermute x3, starting transfers between devices, body(): lax.ppermute(atom_pack, 'mp', [(m, (m + shift) % MP) for m in range(MP)])  7.81 us
    ppermute x1, waiting for transfers between devices, body(): lax.ppermute(edge_feat, 'edge', [(e, e ^ half) for e in range(OWNERS)])  4.62 us
  transfers between devices with their start and end apart: 7, of which 6 were waited for; matrix products, arithmetic and copies ran while one was open for 0% of the time, Pallas kernels for 3%

profile of v6, /device:TPU:1, one launch (start us, length us, event | category | flops | bytes accessed | tf_op | source)
XLA Modules:
  0.0 142.2 jit_solution(17488678171030751037)
XLA Ops:
  0.0 0.0 copy-start
  0.0 11.6 %collective-permute-start = (bf16[2048,128]{1,0:T(8,128)(2,1)}, bf16[2048,128]{1,0:T(8,128)(2,1)S(1)}, u32[]{:S(2)}, u32[]{:S(2)}) collective-permute-start(bf16[2048,128]{1,0:T(8,128)(2,1)} %param.12), channel_id=1, source_target_pairs={{0,256},{4,260},{8,264},{12,268},{16,272},{20,276},{24,280},{28,28... | collective-permute-start | bytes 1572872 | tf_op jit(solution)/shard_map/ppermute | solution.py:414
  11.6 2.4 %share_rows_and_weights.1 = bf16[4,1536,128]{2,1,0:T(8,128)(2,1)} custom-call(bf16[4,512,128]{2,1,0:T(8,128)(2,1)} %bitcast.15, bf16[512,128]{1,0:T(8,128)(2,1)} %up_ref.1, bf16[128,512]{1,0:T(8,128)(2,1)} %down_ref.1, bf16[512,128]{1,0:T(8,128)(2,1)} %self_ref.1, bf16[512,128]{1,0:T(8,128)(2,1)} %mirror_ref.1), custom_call_target="tpu_custom_call" | custom-call | tf_op jit(solution)/shard_map/share_rows_and_weights/pallas_call | solution.py:188
  14.0 0.0 copy-start.7
  14.0 4.0 %all-to-all-start = ((bf16[4,1536,128]{2,1,0:T(8,128)(2,1)}), bf16[4,1536,128]{2,1,0:T(8,128)(2,1)S(1)}, u32[]{:S(2)}, u32[]{:S(2)}) async-start(bf16[4,1536,128]{2,1,0:T(8,128)(2,1)} %share_rows_and_weights.1), calls=%async_computation | async-start | bytes 3145728 | tf_op jit(solution)/shard_map/all_to_all | solution.py:396
  18.0 0.0 copy-done
  18.0 4.6 %collective-permute-done.rows_ref = bf16[2048,128]{1,0:T(8,128)(2,1)S(1)} collective-permute-done((bf16[2048,128]{1,0:T(8,128)(2,1)}, bf16[2048,128]{1,0:T(8,128)(2,1)S(1)}, u32[]{:S(2)}, u32[]{:S(2)}) %collective-permute-start) | collective-permute-done | bytes 524320 | tf_op jit(solution)/shard_map/ppermute | solution.py:414
  22.6 0.0 copy-done.7
  22.6 1.3 gather_rows.1.rows_ref
  24.0 13.6 %all-to-all-done.mine_ref = bf16[4,1536,128]{2,1,0:T(8,128)(2,1)S(1)} async-done(((bf16[4,1536,128]{2,1,0:T(8,128)(2,1)}), bf16[4,1536,128]{2,1,0:T(8,128)(2,1)S(1)}, u32[]{:S(2)}, u32[]{:S(2)}) %all-to-all-start) | async-done | bytes 1572896 | tf_op jit(solution)/shard_map/all_to_all | solution.py:396
  37.5 4.0 %collective-permute-start.1 = (bf16[4,1536,128]{2,1,0:T(8,128)(2,1)S(1)}, bf16[4,1536,128]{2,1,0:T(8,128)(2,1)S(1)}, u32[]{:S(2)}, u32[]{:S(2)}) collective-permute-start(bf16[4,1536,128]{2,1,0:T(8,128)(2,1)S(1)} %all-to-all-done.mine_ref), channel_id=1, source_target_pairs={{0,4},{4,0},{8,12},{12,8},{16,20},{20,16},{24,28},{28,24},{32,36},... | collective-permute-start | bytes 4718600 | tf_op jit(solution)/shard_map/ppermute | solution.py:424
  41.6 11.7 %all_to_all.30.rev_ref = bf16[4,512,128]{2,1,0:T(8,128)(2,1)S(1)} all-to-all(bf16[4,512,128]{2,1,0:T(8,128)(2,1)S(1)} %bitcast.9), channel_id=1, replica_groups=mesh['edge'=128,'mp'=4] {'mp'}, dimensions={0} | all-to-all | bytes 1048576 | tf_op jit(solution)/shard_map/all_to_all | solution.py:396
  53.3 0.0 collective-permute-done.1.other_hbm
  53.3 3.2 %edge_stage.1 = bf16[4,256,128]{2,1,0:T(8,128)(2,1)S(1)} custom-call(bf16[4,1536,128]{2,1,0:T(8,128)(2,1)S(1)} %all-to-all-done.mine_ref, bf16[4,1536,128]{2,1,0:T(8,128)(2,1)S(1)} %collective-permute-done.1.other_hbm, bf16[4,512,128]{2,1,0:T(8,128)(2,1)S(1)} %all_to_all.30.rev_ref, s32[1,512]{1,0:T(1,128)S(1)} %bitcast.10), custom_call_target="tpu_custom_call" | custom-call | tf_op jit(solution)/shard_map/edge_stage/pallas_call | solution.py:283
  56.5 7.9 %all_to_all.31 = bf16[4,256,128]{2,1,0:T(8,128)(2,1)S(1)} all-to-all(bf16[4,256,128]{2,1,0:T(8,128)(2,1)S(1)} %edge_stage.1), channel_id=1, replica_groups=mesh['edge'=128,'mp'=4] {'mp'}, dimensions={0} | all-to-all | bytes 524288 | tf_op jit(solution)/shard_map/all_to_all | solution.py:396
  64.5 1.3 place_groups.1
  65.8 1.1 copy-done.1
  66.9 14.7 %all-to-all-start.3 = ((bf16[128,40,128]{2,1,0:T(8,128)(2,1)}), bf16[128,40,128]{2,1,0:T(8,128)(2,1)S(1)}, u32[]{:S(2)}, u32[]{:S(2)}) async-start(bf16[128,40,128]{2,1,0:T(8,128)(2,1)} %copy-done.1), calls=%async_computation.3 | async-start | bytes 2621440 | tf_op jit(solution)/shard_map/all_to_all | solution.py:433
  81.6 0.3 pack_weights.1.refs_0_
  81.9 0.0 copy-start.4
  82.0 2.8 %collective-permute-start.4 = (bf16[1024,128]{1,0:T(8,128)(2,1)S(1)}, bf16[1024,128]{1,0:T(8,128)(2,1)S(1)}, u32[]{:S(2)}, u32[]{:S(2)}) collective-permute-start(bf16[1024,128]{1,0:T(8,128)(2,1)S(1)} %pack_weights.1.refs_0_), channel_id=1, source_target_pairs={{0,3},{1,0},{2,1},{3,2},{4,7},{5,4},{6,5},{7,6},{8,11},{9,8},{10,9... | collective-permute-start | bytes 786440 | tf_op jit(solution)/shard_map/ppermute | solution.py:431
  84.8 3.1 %collective-permute-start.3 = (bf16[1024,128]{1,0:T(8,128)(2,1)S(1)}, bf16[1024,128]{1,0:T(8,128)(2,1)S(1)}, u32[]{:S(2)}, u32[]{:S(2)}) collective-permute-start(bf16[1024,128]{1,0:T(8,128)(2,1)S(1)} %pack_weights.1.refs_0_), channel_id=1, source_target_pairs={{0,2},{1,3},{2,0},{3,1},{4,6},{5,7},{6,4},{7,5},{8,10},{9,11},{10,... | collective-permute-start | bytes 786440 | tf_op jit(solution)/shard_map/ppermute | solution.py:431
  87.9 1.9 %collective-permute-start.2 = (bf16[1024,128]{1,0:T(8,128)(2,1)S(1)}, bf16[1024,128]{1,0:T(8,128)(2,1)S(1)}, u32[]{:S(2)}, u32[]{:S(2)}) collective-permute-start(bf16[1024,128]{1,0:T(8,128)(2,1)S(1)} %pack_weights.1.refs_0_), channel_id=1, source_target_pairs={{0,1},{1,2},{2,3},{3,0},{4,5},{5,6},{6,7},{7,4},{8,9},{9,10},{10,1... | collective-permute-start | bytes 786440 | tf_op jit(solution)/shard_map/ppermute | solution.py:431
  89.8 1.0 collective-permute-done.4.refs_3_
  90.8 4.0 %collective-permute-done.3.refs_2_ = bf16[1024,128]{1,0:T(8,128)(2,1)S(1)} collective-permute-done((bf16[1024,128]{1,0:T(8,128)(2,1)S(1)}, bf16[1024,128]{1,0:T(8,128)(2,1)S(1)}, u32[]{:S(2)}, u32[]{:S(2)}) %collective-permute-start.3) | collective-permute-done | bytes 262176 | tf_op jit(solution)/shard_map/ppermute | solution.py:431
  94.8 6.8 %collective-permute-done.2.refs_1_ = bf16[1024,128]{1,0:T(8,128)(2,1)S(1)} collective-permute-done((bf16[1024,128]{1,0:T(8,128)(2,1)S(1)}, bf16[1024,128]{1,0:T(8,128)(2,1)S(1)}, u32[]{:S(2)}, u32[]{:S(2)}) %collective-permute-start.2) | collective-permute-done | bytes 262176 | tf_op jit(solution)/shard_map/ppermute | solution.py:431
  101.6 16.0 %all-to-all-done.3.got_ref = bf16[128,40,128]{2,1,0:T(8,128)(2,1)S(1)} async-done(((bf16[128,40,128]{2,1,0:T(8,128)(2,1)}), bf16[128,40,128]{2,1,0:T(8,128)(2,1)S(1)}, u32[]{:S(2)}, u32[]{:S(2)}) %all-to-all-start.3) | async-done | bytes 1310752 | tf_op jit(solution)/shard_map/all_to_all | solution.py:433
  117.7 0.9 collect_blocks.1
  118.6 11.6 %all_to_all.32.x_ref = bf16[4,512,128]{2,1,0:T(8,128)(2,1)S(1)} all-to-all(bf16[4,512,128]{2,1,0:T(8,128)(2,1)S(1)} %collect_blocks.1), channel_id=1, replica_groups=mesh['edge'=128,'mp'=4] {'mp'}, dimensions={0} | all-to-all | bytes 1048576 | tf_op jit(solution)/shard_map/all_to_all | solution.py:396
  130.2 0.9 atom_stage.1
  131.1 10.4 %all_to_all.33 = bf16[4,512,128]{2,1,0:T(8,128)(2,1)S(1)} all-to-all(bf16[4,512,128]{2,1,0:T(8,128)(2,1)S(1)} %atom_stage.1), channel_id=1, replica_groups=mesh['edge'=128,'mp'=4] {'mp'}, dimensions={0} | all-to-all | bytes 1048576 | tf_op jit(solution)/shard_map/all_to_all | solution.py:396
  141.5 0.8 copy.14
  (12 shorter events, 0.0 us)
Async XLA Ops:
  0.0 18.0 %copy-start = (s32[16,128]{1,0:T(8,128)S(1)}, s32[16,128]{1,0:T(8,128)}, u32[]{:S(2)}) copy-start(s32[16,128]{1,0:T(8,128)} %param.14) | copy-start | bytes 24580
  0.0 22.6 %collective-permute-start = (bf16[2048,128]{1,0:T(8,128)(2,1)}, bf16[2048,128]{1,0:T(8,128)(2,1)S(1)}, u32[]{:S(2)}, u32[]{:S(2)}) collective-permute-start(bf16[2048,128]{1,0:T(8,128)(2,1)} %param.12), channel_id=1, source_target_pairs={{0,256},{4,260},{8,264},{12,268},{16,272},{20,276},{24,280},{28,28... | collective-permute-start | bytes 1572872 | tf_op jit(solution)/shard_map/ppermute | solution.py:414
  14.0 8.7 %copy-start.7 = (s32[2048]{0:T(1024)S(1)}, s32[2048]{0:T(1024)}, u32[]{:S(2)}) copy-start(s32[2048]{0:T(1024)} %param.13) | copy-start | bytes 24580
  14.0 23.6 %all-to-all-start = ((bf16[4,1536,128]{2,1,0:T(8,128)(2,1)}), bf16[4,1536,128]{2,1,0:T(8,128)(2,1)S(1)}, u32[]{:S(2)}, u32[]{:S(2)}) async-start(bf16[4,1536,128]{2,1,0:T(8,128)(2,1)} %share_rows_and_weights.1), calls=%async_computation | async-start | bytes 3145728 | tf_op jit(solution)/shard_map/all_to_all | solution.py:396
  37.5 15.8 %collective-permute-start.1 = (bf16[4,1536,128]{2,1,0:T(8,128)(2,1)S(1)}, bf16[4,1536,128]{2,1,0:T(8,128)(2,1)S(1)}, u32[]{:S(2)}, u32[]{:S(2)}) collective-permute-start(bf16[4,1536,128]{2,1,0:T(8,128)(2,1)S(1)} %all-to-all-done.mine_ref), channel_id=1, source_target_pairs={{0,4},{4,0},{8,12},{12,8},{16,20},{20,16},{24,28},{28,24},{32,36},... | collective-permute-start | bytes 4718600 | tf_op jit(solution)/shard_map/ppermute | solution.py:424
  53.3 11.1 %copy-start.5 = (s32[64,1]{0,1:T(1,128)S(1)}, s32[64,1]{0,1:T(1,128)}, u32[]{:S(2)}) copy-start(s32[64,1]{0,1:T(1,128)} %param.15) | copy-start | bytes 772
  53.3 11.1 %copy-start.6 = (s32[64]{0:T(128)S(1)}, s32[64]{0:T(128)}, u32[]{:S(2)}) copy-start(s32[64]{0:T(128)} %window_ref.1) | copy-start | bytes 772
  65.8 1.1 copy-start.1
  66.9 14.8 %copy-start.2 = (bf16[512,128]{1,0:T(8,128)(2,1)S(1)}, bf16[512,128]{1,0:T(8,128)(2,1)}, u32[]{:S(2)}) copy-start(bf16[512,128]{1,0:T(8,128)(2,1)} %refs_0_) | copy-start | bytes 393220
  66.9 14.8 %copy-start.3 = (bf16[128,512]{1,0:T(8,128)(2,1)S(1)}, bf16[128,512]{1,0:T(8,128)(2,1)}, u32[]{:S(2)}) copy-start(bf16[128,512]{1,0:T(8,128)(2,1)} %refs_1_) | copy-start | bytes 393220
  66.9 50.8 %all-to-all-start.3 = ((bf16[128,40,128]{2,1,0:T(8,128)(2,1)}), bf16[128,40,128]{2,1,0:T(8,128)(2,1)S(1)}, u32[]{:S(2)}, u32[]{:S(2)}) async-start(bf16[128,40,128]{2,1,0:T(8,128)(2,1)} %copy-done.1), calls=%async_computation.3 | async-start | bytes 2621440 | tf_op jit(solution)/shard_map/all_to_all | solution.py:433
  81.9 48.2 %copy-start.4 = (f32[512]{0:T(512)S(1)}, f32[512]{0:T(512)}, u32[]{:S(2)}) copy-start(f32[512]{0:T(512)} %param.23) | copy-start | bytes 6148
  82.0 8.8 %collective-permute-start.4 = (bf16[1024,128]{1,0:T(8,128)(2,1)S(1)}, bf16[1024,128]{1,0:T(8,128)(2,1)S(1)}, u32[]{:S(2)}, u32[]{:S(2)}) collective-permute-start(bf16[1024,128]{1,0:T(8,128)(2,1)S(1)} %pack_weights.1.refs_0_), channel_id=1, source_target_pairs={{0,3},{1,0},{2,1},{3,2},{4,7},{5,4},{6,5},{7,6},{8,11},{9,8},{10,9... | collective-permute-start | bytes 786440 | tf_op jit(solution)/shard_map/ppermute | solution.py:431
  84.8 10.0 %collective-permute-start.3 = (bf16[1024,128]{1,0:T(8,128)(2,1)S(1)}, bf16[1024,128]{1,0:T(8,128)(2,1)S(1)}, u32[]{:S(2)}, u32[]{:S(2)}) collective-permute-start(bf16[1024,128]{1,0:T(8,128)(2,1)S(1)} %pack_weights.1.refs_0_), channel_id=1, source_target_pairs={{0,2},{1,3},{2,0},{3,1},{4,6},{5,7},{6,4},{7,5},{8,10},{9,11},{10,... | collective-permute-start | bytes 786440 | tf_op jit(solution)/shard_map/ppermute | solution.py:431
  87.9 13.8 %collective-permute-start.2 = (bf16[1024,128]{1,0:T(8,128)(2,1)S(1)}, bf16[1024,128]{1,0:T(8,128)(2,1)S(1)}, u32[]{:S(2)}, u32[]{:S(2)}) collective-permute-start(bf16[1024,128]{1,0:T(8,128)(2,1)S(1)} %pack_weights.1.refs_0_), channel_id=1, source_target_pairs={{0,1},{1,2},{2,3},{3,0},{4,5},{5,6},{6,7},{7,4},{8,9},{9,10},{10,1... | collective-permute-start | bytes 786440 | tf_op jit(solution)/shard_map/ppermute | solution.py:431
